TPU v7x, 32 devices: a whole 2x2x4 slice. The times are simulated.
32 devices in a mesh: dp: 8 (over z, x), mp: 4 (over y, core).
Axes of the slice: x: 2, y: 2, z: 4, core: 2. Of those that a mesh axis runs over, the one named last changes fastest.
Arguments:
- states: bfloat16 [16, 512, 1024], P('dp'), may hold values from -36 to 36
- retrieval: float32 [16], P('dp'), may hold values from -15 to 315
- pair_query: int32 [16], replicated, may hold values from 0 to 1, as said below
- positions: int32 [16, 64], P('dp'), may hold values from 0 to 511
- targets: int32 [16, 64], P('dp'), may hold values from 0 to 16383
- proj_weight: bfloat16 [3, 1024, 1024], P(None, None, 'mp'), may hold values from -0.1875 to 0.1875
- out_weight: bfloat16 [1024, 1024], P('mp'), may hold values from -0.1875 to 0.1875
- up_weight: bfloat16 [1024, 4096], P(None, 'mp'), may hold values from -0.1875 to 0.1875
- down_weight: bfloat16 [4096, 1024], P('mp'), may hold values from -0.09375 to 0.09375
- vocab_embed: bfloat16 [16384, 1024], P('mp'), may hold values from -3 to 3
Outputs:
- proj_grad: float32 [3, 1024, 1024], P(None, 'dp', 'mp')
- out_grad: float32 [1024, 1024], P('mp', 'dp')
- up_grad: float32 [1024, 4096], P('dp', 'mp')
- down_grad: float32 [4096, 1024], P('mp', 'dp')
- score_grad: float32 [16], P('dp')
Inputs may be any that keep to these rules, and one draw needn't show every extreme that they name: `pair_query`: each query has 4 to 12 pairs and some query has exactly 12; pairs of one query lie anywhere.
All inputs are finite; a program needn't handle non-finite values.
Results may differ from a plain program's by a relative error of at most 0.019.
Values may be sent and summed in bfloat16 or wider, within the bound.
A program may use at most 192 MiB of HBM per device.

v0:
```python
import jax
import jax.numpy as jnp
from jax import lax
from jax.sharding import PartitionSpec as P

HEAD = 64


def round_trip(value):
    return lax.optimization_barrier(value.astype(jnp.bfloat16)).astype(jnp.float32)


def matmul(left, right):
    return jnp.dot(left, right, preferred_element_type=jnp.float32)


def matmul_tn(left, right):
    return lax.dot_general(
        left, right, (((0,), (0,)), ((), ())), preferred_element_type=jnp.float32
    )


def matmul_nt(left, right):
    return lax.dot_general(
        left, right, (((1,), (1,)), ((), ())), preferred_element_type=jnp.float32
    )


def layer_norm(value):
    centre = jnp.mean(value, axis=-1, keepdims=True)
    centred = value - centre
    spread = jnp.mean(centred * centred, axis=-1, keepdims=True)
    return centred * lax.rsqrt(spread + 1e-05)


def norm_back(value, cotangent):
    return jax.vjp(layer_norm, value)[1](cotangent)[0]


def gelu_tanh(value):
    return jax.nn.gelu(value, approximate=True)


def gelu_back(value, cotangent):
    return jax.vjp(gelu_tanh, value)[1](cotangent)[0]


def attention(projected):
    seq_len = projected.shape[1]
    head_count = projected.shape[2] // HEAD
    parts = projected.astype(jnp.float32).reshape(3, seq_len, head_count, HEAD)
    scores = jnp.einsum("qhd,khd->hqk", parts[0], parts[1]) * HEAD ** (-0.5)
    top_value = jnp.max(scores, axis=-1, keepdims=True)
    weights = jnp.exp(scores - top_value)
    probs = round_trip(weights / jnp.sum(weights, axis=-1, keepdims=True))
    context = jnp.einsum("hqk,khd->qhd", probs, parts[2])
    return context.reshape(seq_len, head_count * HEAD)


def attention_back(projected, cotangent):
    return jax.vjp(attention, projected)[1](cotangent.astype(jnp.float32))[0]


def masked_max(values, member):
    return jnp.max(jnp.where(member, values[:, None], -1e30), axis=0)


def masked_sum(values, member, top_value):
    shifted = jnp.where(member, values[:, None] - top_value[None, :], -1e30)
    return jnp.sum(jnp.where(member, jnp.exp(shifted), 0.0), axis=0)


def per_pair(per_query, member):
    return jnp.sum(jnp.where(member, per_query[None, :], 0.0), axis=1)


def local(
    states,
    retrieval,
    pair_query,
    positions,
    targets,
    proj_weight,
    out_weight,
    up_weight,
    down_weight,
    vocab_embed,
):
    pairs_dev, seq_len, model_width = states.shape
    row_count = pairs_dev * seq_len
    flat_rows = states.reshape(row_count, model_width)
    share_rows = row_count // lax.axis_size("mp")
    row_start = lax.axis_index("mp") * share_rows

    def own_rows(full):
        return lax.dynamic_slice_in_dim(full, row_start, share_rows, 0)

    def reduce_rows(partial_value):
        return lax.psum_scatter(partial_value, "mp", scatter_dimension=0, tiled=True)

    def spread_rows(piece):
        return lax.all_gather(piece, "mp", axis=0, tiled=True)

    projected = jnp.stack(
        [matmul(flat_rows, proj_weight[part_num]) for part_num in range(3)]
    ).astype(jnp.bfloat16)
    grouped = projected.reshape(3, pairs_dev, seq_len, -1)
    context = jax.vmap(attention, in_axes=1)(grouped).reshape(row_count, -1).astype(jnp.bfloat16)
    pre_one = own_rows(flat_rows).astype(jnp.float32) + reduce_rows(matmul(context, out_weight))
    first_own = layer_norm(pre_one).astype(jnp.bfloat16)
    first_norm = spread_rows(first_own)
    inner_act = matmul(first_norm, up_weight)
    activated = gelu_tanh(inner_act).astype(jnp.bfloat16)
    pre_two = first_own.astype(jnp.float32) + reduce_rows(matmul(activated, down_weight))
    final_norm = spread_rows(layer_norm(pre_two).astype(jnp.bfloat16))
    mask_count = positions.shape[1]
    picked = jnp.take_along_axis(
        final_norm.reshape(pairs_dev, seq_len, model_width), positions[:, :, None], axis=1
    ).reshape(-1, model_width)
    logits = matmul_nt(picked, vocab_embed)
    vocab_local = vocab_embed.shape[0]
    local_target = targets.reshape(-1) - lax.axis_index("mp") * vocab_local
    target_hot = local_target[:, None] == jnp.arange(vocab_local)[None, :]
    top_value = lax.pmax(jnp.max(logits, axis=1), "mp")
    exp_terms = jnp.exp(logits - top_value[:, None])
    denominator, target_logit = lax.psum(
        (jnp.sum(exp_terms, axis=1), jnp.sum(jnp.where(target_hot, logits, 0.0), axis=1)), "mp"
    )
    log_prob = target_logit - top_value - jnp.log(denominator)
    doc_ll = jnp.sum(log_prob.reshape(pairs_dev, mask_count), axis=1) / mask_count
    post_values = retrieval + doc_ll
    query_count = pairs_dev * lax.axis_size("dp") // 8
    local_query = lax.dynamic_slice_in_dim(
        pair_query, lax.axis_index("dp") * pairs_dev, pairs_dev, 0
    )
    member = local_query[:, None] == jnp.arange(query_count)[None, :]
    post_top, prior_top = lax.pmax(
        (masked_max(post_values, member), masked_max(retrieval, member)), "dp"
    )
    post_total, prior_total = lax.psum(
        (masked_sum(post_values, member, post_top), masked_sum(retrieval, member, prior_top)), "dp"
    )
    post_lse = post_top + jnp.log(post_total)
    prior_lse = prior_top + jnp.log(prior_total)
    posterior = jnp.exp(post_values - per_pair(post_lse, member))
    prior = jnp.exp(retrieval - per_pair(prior_lse, member))
    score_grad = prior - posterior
    weight_rows = jnp.repeat(posterior, mask_count)
    probs = exp_terms / denominator[:, None]
    dlogit = (weight_rows[:, None] / mask_count * (probs - target_hot.astype(jnp.float32))).astype(
        jnp.bfloat16
    )
    dpicked = lax.psum(matmul(dlogit, vocab_embed), "mp")
    place_hot = (positions[:, :, None] == jnp.arange(seq_len)[None, None, :]).astype(jnp.float32)
    dfinal = jnp.einsum(
        "pms,pmd->psd",
        place_hot,
        dpicked.reshape(pairs_dev, mask_count, model_width),
        precision=lax.Precision.HIGHEST,
    ).reshape(row_count, model_width)
    dpre_own = norm_back(pre_two, own_rows(dfinal)).astype(jnp.bfloat16)
    dpre_two = spread_rows(dpre_own)
    down_term = matmul_tn(activated, dpre_two)
    dinner = gelu_back(inner_act, matmul_nt(dpre_two, down_weight)).astype(jnp.bfloat16)
    up_term = matmul_tn(first_norm, dinner)
    dfirst = dpre_own.astype(jnp.float32) + reduce_rows(matmul_nt(dinner, up_weight))
    dpre_one = spread_rows(norm_back(pre_one, dfirst).astype(jnp.bfloat16))
    out_term = matmul_tn(context, dpre_one)
    dcontext = matmul_nt(dpre_one, out_weight).astype(jnp.bfloat16)
    dgrouped = jax.vmap(attention_back, in_axes=(1, 0), out_axes=1)(
        grouped, dcontext.reshape(pairs_dev, seq_len, -1)
    )
    dprojected = dgrouped.reshape(3, row_count, -1)
    proj_term = jnp.stack([matmul_tn(flat_rows, dprojected[part_num]) for part_num in range(3)])
    proj_grad, out_grad, up_grad, down_grad = (
        lax.psum_scatter(proj_term, "dp", scatter_dimension=1, tiled=True),
        lax.psum_scatter(out_term, "dp", scatter_dimension=1, tiled=True),
        lax.psum_scatter(up_term, "dp", scatter_dimension=0, tiled=True),
        lax.psum_scatter(down_term, "dp", scatter_dimension=1, tiled=True),
    )
    return (proj_grad, out_grad, up_grad, down_grad, score_grad)


def solution(mesh):
    return jax.shard_map(
        local,
        mesh=mesh,
        in_specs=(
            P("dp", None, None),
            P("dp"),
            P(),
            P("dp", None),
            P("dp", None),
            P(None, None, "mp"),
            P("mp", None),
            P(None, "mp"),
            P("mp", None),
            P("mp", None),
        ),
        out_specs=(P(None, "dp", "mp"), P("mp", "dp"), P("dp", "mp"), P("mp", "dp"), P("dp")),
        check_vma=False,
    )
```

profile of v0, /device:TPU:0, one launch (start us, length us, event | category | flops | bytes accessed | tf_op | source)
XLA Modules:
  0.0 766.0 jit_solution(14330715867887948322)
XLA Ops:
  7.2 2.6 fusion.24
  18.8 4.2 convert_reduce_fusion
  27.2 2.7 fusion.64
  30.0 47.3 %reduce-scatter.8.cloned.1.call-done = f32[256,1024]{1,0:T(8,128)} async-done(((f32[1024,1024]{1,0:T(8,128)}), f32[256,1024]{1,0:T(8,128)}) %reduce-scatter.8.cloned.1.call-update) | async-done | bytes 1048592 | tf_op jit(solution)/shard_map/reduce_scatter | solution.py:99
  80.4 22.5 %all-gather.5.cloned.1.call-done = bf16[1024,1024]{1,0:T(8,128)(2,1)} async-done(((bf16[256,1024]{1,0:T(8,128)(2,1)}), bf16[1024,1024]{1,0:T(8,128)(2,1)}) %all-gather.5.cloned.1.call-update) | async-done | bytes 2097168 | tf_op jit(solution)/shard_map/all_gather | solution.py:102
  102.9 4.5 fusion.65
  109.4 4.6 fusion.56
  114.1 44.6 %reduce-scatter.10.cloned.1.call-done = f32[256,1024]{1,0:T(8,128)} async-done(((f32[1024,1024]{1,0:T(8,128)}), f32[256,1024]{1,0:T(8,128)}) %reduce-scatter.10.cloned.1.call-update) | async-done | bytes 1048592 | tf_op jit(solution)/shard_map/reduce_scatter | solution.py:99
  163.4 22.3 %all-gather.7.cloned.1.call-done = bf16[1024,1024]{1,0:T(8,128)(2,1)} async-done(((bf16[256,1024]{1,0:T(8,128)(2,1)}), bf16[1024,1024]{1,0:T(8,128)(2,1)}) %all-gather.7.cloned.1.call-update) | async-done | bytes 2097168 | tf_op jit(solution)/shard_map/all_gather | solution.py:102
  188.0 7.7 fusion.63
  195.7 5.9 pmax.21
  203.8 5.7 all-reduce.5
  209.8 21.5 %all-reduce.4 = (f32[2]{0:T(128)S(1)}, f32[2]{0:T(128)S(1)}) all-reduce(f32[2]{0:T(128)S(1)} %get-tuple-element.26, f32[2]{0:T(128)S(1)} %get-tuple-element.27), channel_id=1, replica_groups=mesh['dp'=8,'mp'=4] {'dp'}, use_global_device_ids=true, to_apply=%region_34.35 | all-reduce | flops 4 | bytes 32 | tf_op jit(solution)/shard_map/pmax | solution.py:137
  231.4 17.1 %all-reduce.3 = (f32[2]{0:T(128)S(1)}, f32[2]{0:T(128)S(1)}) all-reduce(f32[2]{0:T(128)S(1)} %get-tuple-element.24, f32[2]{0:T(128)S(1)} %get-tuple-element.25), channel_id=1, replica_groups=mesh['dp'=8,'mp'=4] {'dp'}, use_global_device_ids=true, to_apply=%region_36.37 | all-reduce | flops 4 | bytes 32 | tf_op jit(solution)/shard_map/psum | solution.py:140
  249.4 6.4 fusion.27
  256.1 32.0 %all-reduce.8.cloned.1.call-done = f32[2,64,1024]{2,1,0:T(8,128)} async-done(((f32[2,64,1024]{2,1,0:T(8,128)}), f32[2,64,1024]{2,1,0:T(8,128)}) %all-reduce.8.cloned.1.call-update) | async-done | bytes 524304 | tf_op jit(solution)/shard_map/psum | solution.py:153
  288.1 3.1 fusion.44
  294.1 22.7 %all-gather.9.cloned.1.call-done = bf16[1024,1024]{1,0:T(8,128)(2,1)} async-done(((bf16[256,1024]{1,0:T(8,128)(2,1)}), bf16[1024,1024]{1,0:T(8,128)(2,1)}) %all-gather.9.cloned.1.call-update) | async-done | bytes 2097168 | tf_op jit(solution)/shard_map/all_gather | solution.py:102
  316.8 7.2 fusion.12
  325.4 4.3 fusion.66
  329.7 44.6 %reduce-scatter.12.cloned.1.call-done = f32[256,1024]{1,0:T(8,128)} async-done(((f32[1024,1024]{1,0:T(8,128)}), f32[256,1024]{1,0:T(8,128)}) %reduce-scatter.12.cloned.1.call-update) | async-done | bytes 1048592 | tf_op jit(solution)/shard_map/reduce_scatter | solution.py:99
  378.9 22.4 %all-gather.11.cloned.1.call-done = bf16[1024,1024]{1,0:T(8,128)(2,1)} async-done(((bf16[256,1024]{1,0:T(8,128)(2,1)}), bf16[1024,1024]{1,0:T(8,128)(2,1)}) %all-gather.11.cloned.1.call-update) | async-done | bytes 2097168 | tf_op jit(solution)/shard_map/all_gather | solution.py:102
  404.3 3.6 convolution_bitcast_fusion.3
  410.4 4.8 fusion.3
  423.1 2.7 copy.51
  432.1 6.9 fusion.55
  440.6 5.9 fusion.68
  447.6 3.3 fusion.67
  450.9 55.7 %reduce-scatter.14.cloned.1.call-done = f32[3,128,256]{1,2,0:T(8,128)} async-done(((f32[3,1024,256]{1,2,0:T(8,128)}), f32[3,128,256]{1,2,0:T(8,128)}) %reduce-scatter.14.cloned.1.call-update) | async-done | bytes 393232 | tf_op jit(solution)/shard_map/reduce_scatter | solution.py:176
  508.5 90.2 %reduce-scatter.20.cloned.1.call-done = f32[1024,128]{1,0:T(8,128)} async-done(((f32[1024,1024]{1,0:T(8,128)}), f32[1024,128]{1,0:T(8,128)}) %reduce-scatter.20.cloned.1.call-update) | async-done | bytes 524304 | tf_op jit(solution)/shard_map/reduce_scatter | solution.py:179
  598.7 92.0 %reduce-scatter.18.cloned.1.call-done = f32[128,1024]{1,0:T(8,128)} async-done(((f32[1024,1024]{1,0:T(8,128)}), f32[128,1024]{1,0:T(8,128)}) %reduce-scatter.18.cloned.1.call-update) | async-done | bytes 524304 | tf_op jit(solution)/shard_map/reduce_scatter | solution.py:178
  690.7 67.9 %reduce-scatter.16.cloned.1.call-done = f32[256,128]{1,0:T(8,128)} async-done(((f32[256,1024]{1,0:T(8,128)}), f32[256,128]{1,0:T(8,128)}) %reduce-scatter.16.cloned.1.call-update) | async-done | bytes 131088 | tf_op jit(solution)/shard_map/reduce_scatter | solution.py:177
  (144 shorter events, 62.0 us)
Async XLA Ops:
  7.2 102.2 %copy-start = (bf16[1024,1024]{1,0:T(8,128)(2,1)S(1)}, bf16[1024,1024]{1,0:T(8,128)(2,1)}, u32[]{:S(2)}) copy-start(bf16[1024,1024]{1,0:T(8,128)(2,1)} %param.18) | copy-start | bytes 6291460
  7.2 70.1 %reduce-scatter.8.cloned.1.call-start = ((), (), s32[]{:S(2)}) async-start(), calls=%async_computation.7 | async-start | bytes 5242880 | tf_op jit(solution)/shard_map/reduce_scatter | solution.py:99
  7.2 5.0 copy-start.6
  14.3 8.7 %copy-start.11 = (bf16[3,2,512,256]{2,3,1,0:T(8,128)(2,1)}, bf16[3,2,512,256]{2,3,1,0:T(8,128)(2,1)S(1)}, u32[]{:S(2)}) copy-start(bf16[3,2,512,256]{2,3,1,0:T(8,128)(2,1)S(1)} %pad_maximum_fusion.1) | copy-start | bytes 4718596
  15.6 3.2 copy-start.2
  23.0 4.2 copy-start.15
  29.9 72.9 %all-gather.5.cloned.1.call-start = ((), (), s32[]{:S(2)}) async-start(), calls=%async_computation.8 | async-start | bytes 2621440 | tf_op jit(solution)/shard_map/all_gather | solution.py:102
  80.1 78.5 %reduce-scatter.10.cloned.1.call-start = ((), (), s32[]{:S(2)}) async-start(), calls=%async_computation.9 | async-start | bytes 5242880 | tf_op jit(solution)/shard_map/reduce_scatter | solution.py:99
  114.0 49.0 %copy-start.18 = (s32[2,64]{1,0:T(2,128)S(1)}, s32[2,64]{1,0:T(2,128)}, u32[]{:S(2)}) copy-start(s32[2,64]{1,0:T(2,128)} %param.14) | copy-start | bytes 1540
  114.0 49.1 %copy-start.17 = (s32[2,64]{1,0:T(2,128)S(1)}, s32[2,64]{1,0:T(2,128)}, u32[]{:S(2)}) copy-start(s32[2,64]{1,0:T(2,128)} %param.13) | copy-start | bytes 1540
  114.0 49.3 %copy-start.22 = (s32[16]{0:T(128)S(1)}, s32[16]{0:T(128)}, u32[]{:S(2)}) copy-start(s32[16]{0:T(128)} %param.12) | copy-start | bytes 196
  114.0 71.7 %all-gather.7.cloned.1.call-start = ((), (), s32[]{:S(2)}) async-start(), calls=%async_computation.10 | async-start | bytes 2621440 | tf_op jit(solution)/shard_map/all_gather | solution.py:102
  158.6 3.2 copy-start.4
  163.0 125.1 %all-reduce.8.cloned.1.call-start = ((), (), s32[]{:S(2)}) async-start(), calls=%async_computation.11 | async-start | bytes 1048576 | tf_op jit(solution)/shard_map/psum | solution.py:153
  188.0 21.7 %copy-start.16 = (f32[2]{0:T(128)S(1)}, f32[2]{0:T(128)}, u32[]{:S(2)}) copy-start(f32[2]{0:T(128)} %param.11) | copy-start | bytes 28
  255.8 61.0 %all-gather.9.cloned.1.call-start = ((), (), s32[]{:S(2)}) async-start(), calls=%async_computation.12 | async-start | bytes 2621440 | tf_op jit(solution)/shard_map/all_gather | solution.py:102
  288.1 3.1 copy-start.5
  294.1 80.3 %reduce-scatter.12.cloned.1.call-start = ((), (), s32[]{:S(2)}) async-start(), calls=%async_computation.13 | async-start | bytes 5242880 | tf_op jit(solution)/shard_map/reduce_scatter | solution.py:99
  316.8 8.6 %copy-start.19 = (bf16[1024,1024]{1,0:T(8,128)(2,1)S(1)}, bf16[1024,1024]{1,0:T(8,128)(2,1)}, u32[]{:S(2)}) copy-start(bf16[1024,1024]{1,0:T(8,128)(2,1)} %param.17) | copy-start | bytes 6291460
  329.7 44.7 %copy-start.10 = (f32[256,1024]{1,0:T(8,128)S(1)}, f32[256,1024]{1,0:T(8,128)}, u32[]{:S(2)}) copy-start(f32[256,1024]{1,0:T(8,128)} %copy-done.9) | copy-start | bytes 3145732
  329.7 71.6 %all-gather.11.cloned.1.call-start = ((), (), s32[]{:S(2)}) async-start(), calls=%async_computation.14 | async-start | bytes 2621440 | tf_op jit(solution)/shard_map/all_gather | solution.py:102
  378.5 128.1 %reduce-scatter.14.cloned.1.call-start = ((), (), s32[]{:S(2)}) async-start(), calls=%async_computation.15 | async-start | bytes 3538944 | tf_op jit(solution)/shard_map/reduce_scatter | solution.py:176
  407.9 7.3 slice-start
  410.4 4.8 slice-start.1
  415.2 2.6 copy-start.8
  415.2 2.6 copy-start.12
  423.1 4.2 copy-start.7
  429.5 2.6 copy-start.21
  431.4 167.2 %reduce-scatter.20.cloned.1.call-start = ((), (), s32[]{:S(2)}) async-start(), calls=%async_computation.18 | async-start | bytes 4718592 | tf_op jit(solution)/shard_map/reduce_scatter | solution.py:179
  439.0 251.7 %reduce-scatter.18.cloned.1.call-start = ((), (), s32[]{:S(2)}) async-start(), calls=%async_computation.17 | async-start | bytes 4718592 | tf_op jit(solution)/shard_map/reduce_scatter | solution.py:178
  446.5 312.1 %copy-start.1 = (bf16[1024,1024]{1,0:T(8,128)(2,1)S(1)}, bf16[1024,1024]{1,0:T(8,128)(2,1)}, u32[]{:S(2)}) copy-start(bf16[1024,1024]{1,0:T(8,128)(2,1)} %param.18) | copy-start | bytes 6291460
  446.6 312.1 %reduce-scatter.16.cloned.1.call-start = ((), (), s32[]{:S(2)}) async-start(), calls=%async_computation.16 | async-start | bytes 1179648 | tf_op jit(solution)/shard_map/reduce_scatter | solution.py:177
  (7 other events, 9.8 us)
Sparse Core Ops, SparseCore 0:
  30.1 47.2 reduce-scatter.7
  80.3 22.5 all-gather.4
  114.1 44.4 reduce-scatter.9
  163.1 22.5 all-gather.6
  255.9 32.0 all-reduce.7
  294.2 22.5 all-gather.8
  329.8 44.4 reduce-scatter.11
  378.7 22.5 all-gather.10
  431.6 75.0 reduce-scatter.13
  511.1 87.5 reduce-scatter.19
  602.9 87.7 reduce-scatter.17
  694.9 63.6 reduce-scatter.15
where the time goes:
time: 773 us; the launch traced here: 766 us
  waiting for transfers between devices  564 us (73%)
  matrix products  80.1 us (10%)
  blocking collectives  50.2 us (6%)
  other arithmetic  32.8 us (4%)
  local copies, waits for them, and re-layouts  21.9 us (3%)
  between operations  15.2 us (2%)
    reduce_scatter x3, waiting for transfers between devices, reduce_rows(): lax.psum_scatter(partial_value, 'mp', scatter_dimension=0, tiled=True)  136 us
    reduce_scatter x1, waiting for transfers between devices, local(): lax.psum_scatter(up_term, 'dp', scatter_dimension=0, tiled=True)  92 us
    reduce_scatter x1, waiting for transfers between devices, local(): lax.psum_scatter(down_term, 'dp', scatter_dimension=1, tiled=True)  90.2 us
    all_gather x4, waiting for transfers between devices, spread_rows(): return lax.all_gather(piece, 'mp', axis=0, tiled=True)  89.9 us
    reduce_scatter x1, waiting for transfers between devices, local(): lax.psum_scatter(out_term, 'dp', scatter_dimension=1, tiled=True)  67.9 us
    reduce_scatter x1, waiting for transfers between devices, local(): lax.psum_scatter(proj_term, 'dp', scatter_dimension=1, tiled=True)  55.7 us
    psum x1, waiting for transfers between devices, local(): dpicked = lax.psum(matmul(dlogit, vocab_embed), 'mp')  32 us
    dot_general x7, matrix products, matmul(): return jnp.dot(left, right, preferred_element_type=jnp.float32)  25.1 us
  transfers between devices with their start and end apart: 12, of which 12 were waited for; matrix products, arithmetic and copies ran while one was open for 2% of the time, Pallas kernels for 0%

commit v1 on v0

v1 whole, which is shorter than its diff:
```python
import jax
import jax.numpy as jnp
from jax import lax
from jax.sharding import PartitionSpec as P

HEAD = 64


def matmul(left, right):
    return jnp.dot(left, right, preferred_element_type=jnp.float32)


def matmul_tn(left, right):
    return lax.dot_general(
        left, right, (((0,), (0,)), ((), ())), preferred_element_type=jnp.float32
    )


def matmul_nt(left, right):
    return lax.dot_general(
        left, right, (((1,), (1,)), ((), ())), preferred_element_type=jnp.float32
    )


def layer_norm(value):
    centre = jnp.mean(value, axis=-1, keepdims=True)
    centred = value - centre
    spread = jnp.mean(centred * centred, axis=-1, keepdims=True)
    return centred * lax.rsqrt(spread + 1e-05)


def norm_back(value, cotangent):
    return jax.vjp(layer_norm, value)[1](cotangent)[0]


def gelu_tanh(value):
    return jax.nn.gelu(value, approximate=True)


def gelu_back(value, cotangent):
    return jax.vjp(gelu_tanh, value)[1](cotangent)[0]


def axis_bits(axis):
    return lax.axis_size(axis).bit_length() - 1


def swap(value, axis, bit):
    pairs = [(i, i ^ (1 << bit)) for i in range(lax.axis_size(axis))]
    return lax.ppermute(value, axis, pairs)


def sum_over_mp(value):
    for bit in range(axis_bits("mp")):
        sent = value.astype(jnp.bfloat16)
        value = sent.astype(jnp.float32) + swap(sent, "mp", bit).astype(jnp.float32)
    return value


def merge_totals(first, second):
    top = jnp.maximum(first[0], second[0])
    total = first[1] * jnp.exp(first[0] - top) + second[1] * jnp.exp(second[0] - top)
    return top, total


def reverse_blocks(value):
    bits = axis_bits("dp")
    rows, width = value.shape
    split = value.reshape(rows, *([2] * bits), width >> bits)
    order = (0, *range(bits, 0, -1), bits + 1)
    return split.transpose(order).reshape(rows, width)


def scatter_sum(compute, value, axis):
    index = lax.axis_index("dp")
    width = value.shape[1] // 2
    bit = index & 1
    sent = compute(lax.dynamic_slice_in_dim(value, (1 - bit) * width, width, 1))
    received = swap(sent.astype(jnp.bfloat16), "dp", 0)
    total = compute(lax.dynamic_slice_in_dim(value, bit * width, width, 1))
    total = total + received.astype(jnp.float32)
    for step in range(1, axis_bits("dp")):
        width //= 2
        bit = (index >> step) & 1
        sent = lax.dynamic_slice_in_dim(total, (1 - bit) * width, width, axis)
        received = swap(sent.astype(jnp.bfloat16), "dp", step)
        total = lax.dynamic_slice_in_dim(total, bit * width, width, axis)
        total = total + received.astype(jnp.float32)
    return total


def masked_max(values, member):
    return jnp.max(jnp.where(member, values[:, None], -1e30), axis=0)


def masked_sum(values, member, top_value):
    shifted = jnp.where(member, values[:, None] - top_value[None, :], -1e30)
    return jnp.sum(jnp.where(member, jnp.exp(shifted), 0.0), axis=0)


def per_pair(per_query, member):
    return jnp.sum(jnp.where(member, per_query[None, :], 0.0), axis=1)


def local(
    states,
    retrieval,
    pair_query,
    positions,
    targets,
    proj_weight,
    out_weight,
    up_weight,
    down_weight,
    vocab_embed,
):
    pairs_dev, seq_len, model_width = states.shape
    mask_count = positions.shape[1]
    slots = pairs_dev * mask_count
    heads = proj_weight.shape[2] // HEAD
    flat_rows = states.reshape(pairs_dev * seq_len, model_width)

    place_hot = (positions[:, :, None] == jnp.arange(seq_len)[None, None, :]).astype(jnp.bfloat16)
    picked_states = jnp.einsum(
        "pms,psd->pmd", place_hot, states, preferred_element_type=jnp.float32
    ).astype(jnp.bfloat16).reshape(slots, model_width)

    query = matmul(picked_states, proj_weight[0]).astype(jnp.bfloat16)
    query = query.reshape(pairs_dev, mask_count, heads, HEAD)
    key = matmul(flat_rows, proj_weight[1]).astype(jnp.bfloat16)
    key = key.reshape(pairs_dev, seq_len, heads, HEAD)
    val = matmul(flat_rows, proj_weight[2]).astype(jnp.bfloat16)
    val = val.reshape(pairs_dev, seq_len, heads, HEAD)
    scores = jnp.einsum(
        "pqhd,pkhd->phqk", query, key, preferred_element_type=jnp.float32
    ) * HEAD ** (-0.5)
    weights = jnp.exp(scores - jnp.max(scores, axis=-1, keepdims=True))
    soft = weights / jnp.sum(weights, axis=-1, keepdims=True)
    probs = soft.astype(jnp.bfloat16)
    context = jnp.einsum("phqk,pkhd->pqhd", probs, val, preferred_element_type=jnp.float32)
    context = context.reshape(slots, heads * HEAD).astype(jnp.bfloat16)

    pre_one = picked_states.astype(jnp.float32) + sum_over_mp(matmul(context, out_weight))
    first_norm = layer_norm(pre_one).astype(jnp.bfloat16)
    inner_act = matmul(first_norm, up_weight)
    activated = gelu_tanh(inner_act).astype(jnp.bfloat16)
    pre_two = first_norm.astype(jnp.float32) + sum_over_mp(matmul(activated, down_weight))
    picked = layer_norm(pre_two).astype(jnp.bfloat16)

    logits = matmul_nt(picked, vocab_embed)
    vocab_local = vocab_embed.shape[0]
    local_target = targets.reshape(-1) - lax.axis_index("mp") * vocab_local
    target_hot = local_target[:, None] == jnp.arange(vocab_local)[None, :]
    top_value = jnp.max(logits, axis=1)
    denominator = jnp.sum(jnp.exp(logits - top_value[:, None]), axis=1)
    target_logit = jnp.sum(jnp.where(target_hot, logits, 0.0), axis=1)
    for bit in range(axis_bits("mp")):
        other = swap(jnp.stack([top_value, denominator, target_logit]), "mp", bit)
        top_value, denominator = merge_totals((top_value, denominator), (other[0], other[1]))
        target_logit = target_logit + other[2]
    log_prob = target_logit - top_value - jnp.log(denominator)
    doc_ll = jnp.sum(log_prob.reshape(pairs_dev, mask_count), axis=1) / mask_count

    post_values = retrieval + doc_ll
    query_count = pairs_dev * lax.axis_size("dp") // 8
    local_query = lax.dynamic_slice_in_dim(
        pair_query, lax.axis_index("dp") * pairs_dev, pairs_dev, 0
    )
    member = local_query[:, None] == jnp.arange(query_count)[None, :]
    tops = jnp.stack([masked_max(post_values, member), masked_max(retrieval, member)])
    totals = jnp.stack(
        [masked_sum(post_values, member, tops[0]), masked_sum(retrieval, member, tops[1])]
    )
    for bit in range(axis_bits("dp")):
        other = swap(jnp.stack([tops, totals]), "dp", bit)
        tops, totals = merge_totals((tops, totals), (other[0], other[1]))
    lse = tops + jnp.log(totals)
    posterior = jnp.exp(post_values - per_pair(lse[0], member))
    prior = jnp.exp(retrieval - per_pair(lse[1], member))
    score_grad = prior - posterior

    vocab_probs = jnp.exp(logits - top_value[:, None]) / denominator[:, None]
    dlogit = (vocab_probs - target_hot.astype(jnp.float32)).astype(jnp.bfloat16)
    dpicked = sum_over_mp(matmul(dlogit, vocab_embed))
    dpicked = dpicked * (jnp.repeat(posterior, mask_count)[:, None] / mask_count)

    dpre_two = norm_back(pre_two, dpicked).astype(jnp.bfloat16)
    down_grad = scatter_sum(
        lambda part: matmul_tn(activated, part), reverse_blocks(dpre_two), 1
    )
    dinner = gelu_back(inner_act, matmul_nt(dpre_two, down_weight)).astype(jnp.bfloat16)
    up_grad = scatter_sum(lambda part: matmul_tn(part, dinner), reverse_blocks(first_norm), 0)
    dfirst = dpre_two.astype(jnp.float32) + sum_over_mp(matmul_nt(dinner, up_weight))
    dpre_one = norm_back(pre_one, dfirst).astype(jnp.bfloat16)
    out_grad = scatter_sum(lambda part: matmul_tn(context, part), reverse_blocks(dpre_one), 1)

    dcontext = matmul_nt(dpre_one, out_weight).astype(jnp.bfloat16)
    dcontext = dcontext.reshape(pairs_dev, mask_count, heads, HEAD)
    turned = reverse_blocks(flat_rows)
    dval = jnp.einsum("phqk,pqhd->pkhd", probs, dcontext, preferred_element_type=jnp.float32)
    dval = dval.astype(jnp.bfloat16).reshape(pairs_dev * seq_len, heads * HEAD)
    val_grad = scatter_sum(lambda part: matmul_tn(part, dval), turned, 0)
    dprobs = jnp.einsum("pqhd,pkhd->phqk", dcontext, val, preferred_element_type=jnp.float32)
    dscores = soft * (dprobs - jnp.sum(soft * dprobs, axis=-1, keepdims=True))
    dscores = (dscores * HEAD ** (-0.5)).astype(jnp.bfloat16)
    dkey = jnp.einsum("phqk,pqhd->pkhd", dscores, query, preferred_element_type=jnp.float32)
    dkey = dkey.astype(jnp.bfloat16).reshape(pairs_dev * seq_len, heads * HEAD)
    key_grad = scatter_sum(lambda part: matmul_tn(part, dkey), turned, 0)
    dquery = jnp.einsum("phqk,pkhd->pqhd", dscores, key, preferred_element_type=jnp.float32)
    dquery = dquery.astype(jnp.bfloat16).reshape(slots, heads * HEAD)
    query_grad = scatter_sum(
        lambda part: matmul_tn(part, dquery), reverse_blocks(picked_states), 0
    )
    proj_grad = jnp.stack([query_grad, key_grad, val_grad])
    return (proj_grad, out_grad, up_grad, down_grad, score_grad)


def solution(mesh):
    return jax.shard_map(
        local,
        mesh=mesh,
        in_specs=(
            P("dp", None, None),
            P("dp"),
            P(),
            P("dp", None),
            P("dp", None),
            P(None, None, "mp"),
            P("mp", None),
            P(None, "mp"),
            P("mp", None),
            P("mp", None),
        ),
        out_specs=(P(None, "dp", "mp"), P("mp", "dp"), P("dp", "mp"), P("mp", "dp"), P("dp")),
        check_vma=False,
    )
```

time: 773 us -> 243 us (0.31)
  waiting for transfers between devices: 564 us -> 99.9 us
  blocking collectives: 50.2 us -> 0 us
  starting transfers between devices: 1.43 us -> 37.4 us
  matrix products: 80.1 us -> 53.4 us
  other arithmetic: 32.8 us -> 12.2 us
  local copies, waits for them, and re-layouts: 21.9 us -> 37.9 us
  between operations: 15.2 us -> 1.58 us
    reduce_scatter x7 -> x0, waiting for transfers between devices: 442 us -> none  [the longest x3 136 us: reduce_rows(): lax.psum_scatter(partial_value, 'mp', scatter_dimension=0, tiled=True)]
    ppermute x0 -> x31, waiting for transfers between devices: none -> 99.9 us  [swap(): return lax.ppermute(value, axis, pairs)]
    all_gather x4 -> x0, waiting for transfers between devices: 89.9 us -> none  [spread_rows(): return lax.all_gather(piece, 'mp', axis=0, tiled=True)]
    ppermute x0 -> x31, starting transfers between devices: none -> 37.4 us  [swap(): return lax.ppermute(value, axis, pairs)]
    psum x1 -> x0, waiting for transfers between devices: 32 us -> none  [local(): dpicked = lax.psum(matmul(dlogit, vocab_embed), 'mp')]
    pmax x2 -> x0, blocking collectives: 27.4 us -> none  [the longest x1 21.5 us: local(): lax.pmax((masked_max(post_values, member), masked_max(retrieval, member))...]
    psum x2 -> x0, blocking collectives: 22.8 us -> none  [the longest x1 17.1 us: local(): lax.psum((masked_sum(post_values, member, post_top), masked_sum(retrieval...]
    reduce_sum x5 -> x1, other arithmetic: 15.2 us -> 0.7 us  [local(): denominator = jnp.sum(jnp.exp(logits - top_value[:, None]), axis=1)]
  transfers between devices with their start and end apart: 12 -> 31, of which waited for: 12 -> 22; matrix products, arithmetic and copies ran while one was open for 2% -> 26% of each run, Pallas kernels for 0% -> 0%
where the time goes in v1:
time: 243 us; the launch traced here: 242 us
  waiting for transfers between devices  99.9 us (41%)
  matrix products  53.4 us (22%)
  local copies, waits for them, and re-layouts  37.9 us (16%)
  starting transfers between devices  37.4 us (15%)
  other arithmetic  12.2 us (5%)
    ppermute x31, waiting for transfers between devices, swap(): return lax.ppermute(value, axis, pairs)  99.9 us
    ppermute x31, starting transfers between devices, swap(): return lax.ppermute(value, axis, pairs)  37.4 us
    dot_general x7, matrix products, matmul(): return jnp.dot(left, right, preferred_element_type=jnp.float32)  12 us
    dot_general x12, matrix products, matmul_tn(): lax.dot_general(left, right, (((0,), (0,)), ((), ())), preferred_element_...  11.7 us
    dot_general x4, matrix products, matmul_nt(): lax.dot_general(left, right, (((1,), (1,)), ((), ())), preferred_element_...  10.3 us
    reshape x6, local copies, waits for them, and re-layouts, reverse_blocks(): split = value.reshape(rows, *[2] * bits, width >> bits)  6.75 us
    transpose x1, local copies, waits for them, and re-layouts, reverse_blocks(): return split.transpose(order).reshape(rows, width)  6.21 us
    dot_general x1, matrix products, local(): jnp.einsum('phqk,pqhd->pkhd', dscores, query, preferred_element_type=jnp....  5.68 us
  transfers between devices with their start and end apart: 31, of which 22 were waited for; matrix products, arithmetic and copies ran while one was open for 26% of the time, Pallas kernels for 0%

profile of v1, /device:TPU:0, one launch (start us, length us, event | category | flops | bytes accessed | tf_op | source)
XLA Modules:
  0.0 242.5 jit_solution(7295046781124664669)
XLA Ops:
  0.7 2.5 %convolution_convert_fusion.5 = bf16[1024,256]{1,0:T(8,128)(2,1)S(1)} fusion(bf16[1024,1024]{1,0:T(8,128)(2,1)} %bitcast.230, bf16[3,1024,256]{2,1,0:T(8,128)(2,1)} %param.15), kind=kOutput, calls=%fused_computation.19 | convolution fusion | flops 537133056 | bytes 3145728 | tf_op jit(solution)/shard_map/dot_general | solution.py:10
  20.8 3.0 %collective-permute-start.1 = (bf16[128,1024]{1,0:T(8,128)(2,1)S(1)}, bf16[128,1024]{1,0:T(8,128)(2,1)S(1)}, u32[]{:S(2)}, u32[]{:S(2)}) collective-permute-start(bf16[128,1024]{1,0:T(8,128)(2,1)S(1)} %add_convert_fusion.5), channel_id=1, source_target_pairs={{0,2},{1,3},{2,0},{3,1},{4,6},{5,7},{6,4},{7,5},{8,10},{9,11},{10,... | collective-permute-start | bytes 786440 | tf_op jit(solution)/shard_map/ppermute | solution.py:50
  23.7 6.6 %collective-permute-done.1 = bf16[128,1024]{1,0:T(8,128)(2,1)S(1)} collective-permute-done((bf16[128,1024]{1,0:T(8,128)(2,1)S(1)}, bf16[128,1024]{1,0:T(8,128)(2,1)S(1)}, u32[]{:S(2)}, u32[]{:S(2)}) %collective-permute-start.1) | collective-permute-done | bytes 262176 | tf_op jit(solution)/shard_map/ppermute | solution.py:50
  34.0 1.8 collective-permute-start.3
  35.9 6.5 %collective-permute-done.3 = bf16[128,1024]{1,0:T(8,128)(2,1)S(1)} collective-permute-done((bf16[128,1024]{1,0:T(8,128)(2,1)S(1)}, bf16[128,1024]{1,0:T(8,128)(2,1)S(1)}, u32[]{:S(2)}, u32[]{:S(2)}) %collective-permute-start.3) | collective-permute-done | bytes 262176 | tf_op jit(solution)/shard_map/ppermute | solution.py:50
  43.4 6.4 %fusion.121 = (f32[128]{0:T(128)S(1)}, f32[128,4096]{1,0:T(8,128)S(1)}) fusion(bf16[4096,1024]{1,0:T(8,128)(2,1)} %param.19, f32[128]{0:T(128)S(1)} %fusion.111, f32[128]{0:T(128)S(1)} %broadcast_multiply_fusion.1, bf16[128,1024]{1,0:T(8,128)(2,1)S(1)} %collective-permute-done.3, bf16[128,1024]{1,0:T(8,128)(2,1)S(1)} %add_convert_fusion.4, ...), kind=kOutput, calls=%fused_computation.247 | convolution fusion | flops 1075314560 | bytes 11273728 | tf_op jit(solution)/shard_map/dot_general | solution.py:20
  53.1 1.8 collective-permute-start.5
  60.4 5.6 %convolution_convert_fusion.11 = bf16[128,1024]{1,0:T(8,128)(2,1)S(1)} fusion(bf16[4096,1024]{1,0:T(8,128)(2,1)} %param.19, f32[128,4096]{1,0:T(8,128)} %copy-done.7, f32[128]{0:T(128)S(1)} %get-tuple-element.25, f32[128]{0:T(128)S(1)} %get-tuple-element.26, s32[128]{0:T(128)} %copy-done.38), kind=kOutput, calls=%fused_computation.28 | convolution fusion | flops 1077018624 | bytes 10749440 | tf_op jit(solution)/shard_map/dot_general | solution.py:10
  67.7 2.0 collective-permute-done.9
  69.7 2.6 %collective-permute-start.10 = (f32[2,2,2]{2,1,0:T(2,128)S(1)}, f32[2,2,2]{2,1,0:T(2,128)S(1)}, u32[]{:S(2)}, u32[]{:S(2)}) collective-permute-start(f32[2,2,2]{2,1,0:T(2,128)S(1)} %pad_maximum_fusion.5), channel_id=1, source_target_pairs={{0,16},{4,20},{8,24},{12,28},{16,0},{20,4},{24,8},{28,12},{1,17},{... | collective-permute-start | bytes 104 | tf_op jit(solution)/shard_map/ppermute | solution.py:50
  72.4 1.9 collective-permute-done.10
  77.5 4.3 %collective-permute-done.7 = bf16[128,1024]{1,0:T(8,128)(2,1)} collective-permute-done((bf16[128,1024]{1,0:T(8,128)(2,1)}, bf16[128,1024]{1,0:T(8,128)(2,1)}, u32[]{:S(2)}, u32[]{:S(2)}) %collective-permute-start.7) | collective-permute-done | bytes 262176 | tf_op jit(solution)/shard_map/ppermute | solution.py:50
  88.8 4.5 %reshape_reshape.7 = bf16[1024,2,2,2,128]{4,3,2,1,0:T(2,128)(2,1)} reshape(bf16[2,512,1024]{2,1,0:T(8,128)(2,1)} %param.10) | data formatting | bytes 4194304 | tf_op jit(solution)/shard_map/reshape;reshape | solution.py:69
  94.2 6.2 %copy.71 = bf16[1024,2,2,2,128]{0,4,3,2,1:T(8,128)(2,1)} copy(bf16[1024,2,2,2,128]{4,1,2,3,0:T(2,128)(2,1)} %bitcast.232) | data formatting | bytes 4194304 | tf_op jit(solution)/shard_map/transpose | solution.py:71
  101.3 1.8 copy.77
  108.0 2.4 convolution_convert_fusion
  118.5 2.4 fusion.123
  120.9 5.4 %fusion.11 = bf16[2,64,4,64]{1,3,2,0:T(8,128)(2,1)} fusion(bf16[2,512,4,64]{1,3,2,0:T(8,128)(2,1)S(1)} %copy-done.17, f32[2,4,64,512]{3,2,1,0:T(8,128)} %fusion.123, f32[2,4,64,512]{3,2,1,0:T(8,128)} %get-tuple-element.39, f32[2,4,64]{2,1,0:T(4,128)S(1)} %get-tuple-element.38), kind=kOutput, calls=%fused_computation.35 | convolution fusion | flops 35423232 | bytes 2689024 | tf_op jit(solution)/shard_map/phqk,pkhd->pqhd/dot_general | solution.py:209
  126.3 5.7 %fusion.8 = bf16[2,512,4,64]{1,3,2,0:T(8,128)(2,1)} fusion(bf16[2,64,4,64]{1,3,2,0:T(8,128)(2,1)S(1)} %copy-done.29, f32[2,4,64,512]{3,2,1,0:T(8,128)} %fusion.123, f32[2,4,64,512]{3,2,1,0:T(8,128)} %get-tuple-element.39, f32[2,4,64]{2,1,0:T(4,128)S(1)} %get-tuple-element.38), kind=kOutput, calls=%fused_computation.21 | convolution fusion | flops 35652608 | bytes 2689024 | tf_op jit(solution)/shard_map/phqk,pqhd->pkhd/dot_general | solution.py:206
  132.0 2.5 %fusion.9 = bf16[2,512,4,64]{1,3,2,0:T(8,128)(2,1)} fusion(bf16[2,64,4,64]{1,3,2,0:T(8,128)(2,1)} %copy-done.30, f32[2,4,64]{2,1,0:T(4,128)S(1)} %get-tuple-element.38, bf16[2,64,4,64]{1,3,2,0:T(8,128)(2,1)} %copy.72, bf16[2,512,4,64]{1,3,2,0:T(8,128)(2,1)S(1)} %copy-done.17), kind=kOutput, calls=%fused_computation.22 | convolution fusion | flops 68420608 | bytes 1181696 | tf_op jit(solution)/shard_map/phqk,pqhd->pkhd/dot_general | solution.py:200
  144.0 20.7 %collective-permute-done.22 = bf16[256,512]{1,0:T(8,128)(2,1)} collective-permute-done((bf16[256,512]{1,0:T(8,128)(2,1)}, bf16[256,512]{1,0:T(8,128)(2,1)}, u32[]{:S(2)}, u32[]{:S(2)}) %collective-permute-start.22) | collective-permute-done | bytes 262176 | tf_op jit(solution)/shard_map/ppermute | solution.py:50
  166.5 3.8 %collective-permute-done.13 = bf16[512,256]{1,0:T(8,128)(2,1)S(1)} collective-permute-done((bf16[512,256]{1,0:T(8,128)(2,1)S(1)}, bf16[512,256]{1,0:T(8,128)(2,1)S(1)}, u32[]{:S(2)}, u32[]{:S(2)}) %collective-permute-start.13) | collective-permute-done | bytes 262176 | tf_op jit(solution)/shard_map/ppermute | solution.py:50
  172.1 3.8 %collective-permute-done.16 = bf16[512,256]{1,0:T(8,128)(2,1)S(1)} collective-permute-done((bf16[512,256]{1,0:T(8,128)(2,1)S(1)}, bf16[512,256]{1,0:T(8,128)(2,1)S(1)}, u32[]{:S(2)}, u32[]{:S(2)}) %collective-permute-start.16) | collective-permute-done | bytes 262176 | tf_op jit(solution)/shard_map/ppermute | solution.py:50
  178.0 2.8 %collective-permute-done.19 = bf16[512,256]{1,0:T(8,128)(2,1)S(1)} collective-permute-done((bf16[512,256]{1,0:T(8,128)(2,1)S(1)}, bf16[512,256]{1,0:T(8,128)(2,1)S(1)}, u32[]{:S(2)}, u32[]{:S(2)}) %collective-permute-start.19) | collective-permute-done | bytes 262176 | tf_op jit(solution)/shard_map/ppermute | solution.py:50
  183.5 2.6 %collective-permute-start.24 = (bf16[256,128]{1,0:T(8,128)(2,1)S(1)}, bf16[256,128]{1,0:T(8,128)(2,1)S(1)}, u32[]{:S(2)}, u32[]{:S(2)}) collective-permute-start(bf16[256,128]{1,0:T(8,128)(2,1)S(1)} %dynamic-slice_convert_fusion.8), channel_id=1, source_target_pairs={{0,16},{4,20},{8,24},{12,28},{16,0},{20,4},{24,8},{28,12},{1,17},{... | collective-permute-start | bytes 196616 | tf_op jit(solution)/shard_map/ppermute | solution.py:50
  187.5 1.9 collective-permute-start.15
  196.1 2.1 collective-permute-done.18
  202.0 2.1 collective-permute-start.26
  204.1 13.8 %collective-permute-done.29 = bf16[1024,256]{1,0:T(8,128)(2,1)S(1)} collective-permute-done((bf16[1024,256]{1,0:T(8,128)(2,1)S(1)}, bf16[1024,256]{1,0:T(8,128)(2,1)S(1)}, u32[]{:S(2)}, u32[]{:S(2)}) %collective-permute-start.29) | collective-permute-done | bytes 524320 | tf_op jit(solution)/shard_map/ppermute | solution.py:50
  218.9 10.3 %collective-permute-done.26 = bf16[256,1024]{1,0:T(8,128)(2,1)S(1)} collective-permute-done((bf16[256,1024]{1,0:T(8,128)(2,1)S(1)}, bf16[256,1024]{1,0:T(8,128)(2,1)S(1)}, u32[]{:S(2)}, u32[]{:S(2)}) %collective-permute-start.26) | collective-permute-done | bytes 524320 | tf_op jit(solution)/shard_map/ppermute | solution.py:50
  230.3 6.1 %collective-permute-done.30 = bf16[1024,128]{1,0:T(8,128)(2,1)S(1)} collective-permute-done((bf16[1024,128]{1,0:T(8,128)(2,1)S(1)}, bf16[1024,128]{1,0:T(8,128)(2,1)S(1)}, u32[]{:S(2)}, u32[]{:S(2)}) %collective-permute-start.30) | collective-permute-done | bytes 262176 | tf_op jit(solution)/shard_map/ppermute | solution.py:50
  237.3 4.3 %collective-permute-done.27 = bf16[128,1024]{1,0:T(8,128)(2,1)S(1)} collective-permute-done((bf16[128,1024]{1,0:T(8,128)(2,1)S(1)}, bf16[128,1024]{1,0:T(8,128)(2,1)S(1)}, u32[]{:S(2)}, u32[]{:S(2)}) %collective-permute-start.27) | collective-permute-done | bytes 262176 | tf_op jit(solution)/shard_map/ppermute | solution.py:50
  (250 shorter events, 90.5 us)
Async XLA Ops:
  0.6 31.2 %copy-start = (bf16[1024,1024]{1,0:T(8,128)(2,1)S(1)}, bf16[1024,1024]{1,0:T(8,128)(2,1)}, u32[]{:S(2)}) copy-start(bf16[1024,1024]{1,0:T(8,128)(2,1)} %param.18) | copy-start | bytes 6291460
  19.0 1.7 collective-permute-start
  20.8 9.6 %collective-permute-start.1 = (bf16[128,1024]{1,0:T(8,128)(2,1)S(1)}, bf16[128,1024]{1,0:T(8,128)(2,1)S(1)}, u32[]{:S(2)}, u32[]{:S(2)}) collective-permute-start(bf16[128,1024]{1,0:T(8,128)(2,1)S(1)} %add_convert_fusion.5), channel_id=1, source_target_pairs={{0,2},{1,3},{2,0},{3,1},{4,6},{5,7},{6,4},{7,5},{8,10},{9,11},{10,... | collective-permute-start | bytes 786440 | tf_op jit(solution)/shard_map/ppermute | solution.py:50
  32.4 1.6 collective-permute-start.2
  34.0 8.4 %collective-permute-start.3 = (bf16[128,1024]{1,0:T(8,128)(2,1)S(1)}, bf16[128,1024]{1,0:T(8,128)(2,1)S(1)}, u32[]{:S(2)}, u32[]{:S(2)}) collective-permute-start(bf16[128,1024]{1,0:T(8,128)(2,1)S(1)} %add_convert_fusion.4), channel_id=1, source_target_pairs={{0,2},{1,3},{2,0},{3,1},{4,6},{5,7},{6,4},{7,5},{8,10},{9,11},{10,... | collective-permute-start | bytes 786440 | tf_op jit(solution)/shard_map/ppermute | solution.py:50
  51.9 1.2 collective-permute-start.4
  53.1 3.7 %collective-permute-start.5 = (f32[3,128]{1,0:T(4,128)S(1)}, f32[3,128]{1,0:T(4,128)S(1)}, u32[]{:S(2)}, u32[]{:S(2)}) collective-permute-start(f32[3,128]{1,0:T(4,128)S(1)} %pad_maximum_fusion.2), channel_id=1, source_target_pairs={{0,2},{1,3},{2,0},{3,1},{4,6},{5,7},{6,4},{7,5},{8,10},{9,11},{10,... | collective-permute-start | bytes 4616 | tf_op jit(solution)/shard_map/ppermute | solution.py:50
  58.6 7.5 %collective-permute-start.8 = (f32[2,2,2]{2,1,0:T(2,128)S(1)}, f32[2,2,2]{2,1,0:T(2,128)S(1)}, u32[]{:S(2)}, u32[]{:S(2)}) collective-permute-start(f32[2,2,2]{2,1,0:T(2,128)S(1)} %pad_maximum_fusion.3), channel_id=1, source_target_pairs={{0,4},{4,0},{8,12},{12,8},{16,20},{20,16},{24,28},{28,24},{1,5},{5... | collective-permute-start | bytes 104 | tf_op jit(solution)/shard_map/ppermute | solution.py:50
  65.9 8.4 %collective-permute-start.6 = (bf16[128,1024]{1,0:T(8,128)(2,1)S(1)}, bf16[128,1024]{1,0:T(8,128)(2,1)S(1)}, u32[]{:S(2)}, u32[]{:S(2)}) collective-permute-start(bf16[128,1024]{1,0:T(8,128)(2,1)S(1)} %convolution_convert_fusion.11), channel_id=1, source_target_pairs={{0,1},{1,0},{2,3},{3,2},{4,5},{5,4},{6,7},{7,6},{8,9},{9,8},{10,11... | collective-permute-start | bytes 786440 | tf_op jit(solution)/shard_map/ppermute | solution.py:50
  66.1 3.7 %collective-permute-start.9 = (f32[2,2,2]{2,1,0:T(2,128)S(1)}, f32[2,2,2]{2,1,0:T(2,128)S(1)}, u32[]{:S(2)}, u32[]{:S(2)}) collective-permute-start(f32[2,2,2]{2,1,0:T(2,128)S(1)} %pad_maximum_fusion.4), channel_id=1, source_target_pairs={{0,8},{4,12},{8,0},{12,4},{16,24},{20,28},{24,16},{28,20},{1,9},{5... | collective-permute-start | bytes 104 | tf_op jit(solution)/shard_map/ppermute | solution.py:50
  69.7 4.5 %collective-permute-start.10 = (f32[2,2,2]{2,1,0:T(2,128)S(1)}, f32[2,2,2]{2,1,0:T(2,128)S(1)}, u32[]{:S(2)}, u32[]{:S(2)}) collective-permute-start(f32[2,2,2]{2,1,0:T(2,128)S(1)} %pad_maximum_fusion.5), channel_id=1, source_target_pairs={{0,16},{4,20},{8,24},{12,28},{16,0},{20,4},{24,8},{28,12},{1,17},{... | collective-permute-start | bytes 104 | tf_op jit(solution)/shard_map/ppermute | solution.py:50
  75.1 6.7 %collective-permute-start.7 = (bf16[128,1024]{1,0:T(8,128)(2,1)}, bf16[128,1024]{1,0:T(8,128)(2,1)}, u32[]{:S(2)}, u32[]{:S(2)}) collective-permute-start(bf16[128,1024]{1,0:T(8,128)(2,1)} %add_convert_fusion.3), channel_id=1, source_target_pairs={{0,2},{1,3},{2,0},{3,1},{4,6},{5,7},{6,4},{7,5},{8,10},{9,11},{10,... | collective-permute-start | bytes 786440 | tf_op jit(solution)/shard_map/ppermute | solution.py:50
  88.7 16.5 %collective-permute-start.11 = (bf16[128,1024]{1,0:T(8,128)(2,1)}, bf16[128,1024]{1,0:T(8,128)(2,1)}, u32[]{:S(2)}, u32[]{:S(2)}) collective-permute-start(bf16[128,1024]{1,0:T(8,128)(2,1)} %convolution_convert_fusion.10), channel_id=1, source_target_pairs={{0,1},{1,0},{2,3},{3,2},{4,5},{5,4},{6,7},{7,6},{8,9},{9,8},{10,11... | collective-permute-start | bytes 786440 | tf_op jit(solution)/shard_map/ppermute | solution.py:50
  106.4 8.8 %collective-permute-start.12 = (bf16[128,1024]{1,0:T(8,128)(2,1)S(1)}, bf16[128,1024]{1,0:T(8,128)(2,1)S(1)}, u32[]{:S(2)}, u32[]{:S(2)}) collective-permute-start(bf16[128,1024]{1,0:T(8,128)(2,1)S(1)} %add_convert_fusion.1), channel_id=1, source_target_pairs={{0,2},{1,3},{2,0},{3,1},{4,6},{5,7},{6,4},{7,5},{8,10},{9,11},{10,... | collective-permute-start | bytes 786440 | tf_op jit(solution)/shard_map/ppermute | solution.py:50
  110.3 87.9 %collective-permute-start.28 = (bf16[1024,512]{1,0:T(8,128)(2,1)}, bf16[1024,512]{1,0:T(8,128)(2,1)}, u32[]{:S(2)}, u32[]{:S(2)}) collective-permute-start(bf16[1024,512]{1,0:T(8,128)(2,1)} %convolution_convert_fusion), channel_id=1, source_target_pairs={{0,4},{4,0},{8,12},{12,8},{16,20},{20,16},{24,28},{28,24},{1,5},{5... | collective-permute-start | bytes 3145736 | tf_op jit(solution)/shard_map/ppermute | solution.py:50
  112.3 87.9 %collective-permute-start.25 = (bf16[512,1024]{1,0:T(8,128)(2,1)}, bf16[512,1024]{1,0:T(8,128)(2,1)}, u32[]{:S(2)}, u32[]{:S(2)}) collective-permute-start(bf16[512,1024]{1,0:T(8,128)(2,1)} %convolution_convert_fusion.1), channel_id=1, source_target_pairs={{0,4},{4,0},{8,12},{12,8},{16,20},{20,16},{24,28},{28,24},{1,5},{5... | collective-permute-start | bytes 3145736 | tf_op jit(solution)/shard_map/ppermute | solution.py:50
  136.7 28.1 %collective-permute-start.22 = (bf16[256,512]{1,0:T(8,128)(2,1)}, bf16[256,512]{1,0:T(8,128)(2,1)}, u32[]{:S(2)}, u32[]{:S(2)}) collective-permute-start(bf16[256,512]{1,0:T(8,128)(2,1)} %convolution_convert_fusion.6), channel_id=1, source_target_pairs={{0,4},{4,0},{8,12},{12,8},{16,20},{20,16},{24,28},{28,24},{1,5},{5... | collective-permute-start | bytes 786440 | tf_op jit(solution)/shard_map/ppermute | solution.py:50
  138.6 31.7 %collective-permute-start.13 = (bf16[512,256]{1,0:T(8,128)(2,1)S(1)}, bf16[512,256]{1,0:T(8,128)(2,1)S(1)}, u32[]{:S(2)}, u32[]{:S(2)}) collective-permute-start(bf16[512,256]{1,0:T(8,128)(2,1)S(1)} %convolution_convert_fusion.9), channel_id=1, source_target_pairs={{0,4},{4,0},{8,12},{12,8},{16,20},{20,16},{24,28},{28,24},{1,5},{5... | collective-permute-start | bytes 786440 | tf_op jit(solution)/shard_map/ppermute | solution.py:50
  142.4 33.5 %collective-permute-start.16 = (bf16[512,256]{1,0:T(8,128)(2,1)S(1)}, bf16[512,256]{1,0:T(8,128)(2,1)S(1)}, u32[]{:S(2)}, u32[]{:S(2)}) collective-permute-start(bf16[512,256]{1,0:T(8,128)(2,1)S(1)} %convolution_convert_fusion.8), channel_id=1, source_target_pairs={{0,4},{4,0},{8,12},{12,8},{16,20},{20,16},{24,28},{28,24},{1,5},{5... | collective-permute-start | bytes 786440 | tf_op jit(solution)/shard_map/ppermute | solution.py:50
  164.7 16.0 %collective-permute-start.19 = (bf16[512,256]{1,0:T(8,128)(2,1)S(1)}, bf16[512,256]{1,0:T(8,128)(2,1)S(1)}, u32[]{:S(2)}, u32[]{:S(2)}) collective-permute-start(bf16[512,256]{1,0:T(8,128)(2,1)S(1)} %convolution_convert_fusion.7), channel_id=1, source_target_pairs={{0,4},{4,0},{8,12},{12,8},{16,20},{20,16},{24,28},{28,24},{1,5},{5... | collective-permute-start | bytes 786440 | tf_op jit(solution)/shard_map/ppermute | solution.py:50
  170.3 12.6 %collective-permute-start.23 = (bf16[256,256]{1,0:T(8,128)(2,1)S(1)}, bf16[256,256]{1,0:T(8,128)(2,1)S(1)}, u32[]{:S(2)}, u32[]{:S(2)}) collective-permute-start(bf16[256,256]{1,0:T(8,128)(2,1)S(1)} %dynamic-slice_convert_fusion.4), channel_id=1, source_target_pairs={{0,8},{4,12},{8,0},{12,4},{16,24},{20,28},{24,16},{28,20},{1,9},{5... | collective-permute-start | bytes 393224 | tf_op jit(solution)/shard_map/ppermute | solution.py:50
  175.9 7.6 %collective-permute-start.14 = (bf16[256,256]{1,0:T(8,128)(2,1)S(1)}, bf16[256,256]{1,0:T(8,128)(2,1)S(1)}, u32[]{:S(2)}, u32[]{:S(2)}) collective-permute-start(bf16[256,256]{1,0:T(8,128)(2,1)S(1)} %dynamic-slice_convert_fusion.7), channel_id=1, source_target_pairs={{0,8},{4,12},{8,0},{12,4},{16,24},{20,28},{24,16},{28,20},{1,9},{5... | collective-permute-start | bytes 393224 | tf_op jit(solution)/shard_map/ppermute | solution.py:50
  180.8 6.8 %collective-permute-start.17 = (bf16[256,256]{1,0:T(8,128)(2,1)S(1)}, bf16[256,256]{1,0:T(8,128)(2,1)S(1)}, u32[]{:S(2)}, u32[]{:S(2)}) collective-permute-start(bf16[256,256]{1,0:T(8,128)(2,1)S(1)} %dynamic-slice_convert_fusion.6), channel_id=1, source_target_pairs={{0,8},{4,12},{8,0},{12,4},{16,24},{20,28},{24,16},{28,20},{1,9},{5... | collective-permute-start | bytes 393224 | tf_op jit(solution)/shard_map/ppermute | solution.py:50
  182.9 7.8 %collective-permute-start.20 = (bf16[256,256]{1,0:T(8,128)(2,1)S(1)}, bf16[256,256]{1,0:T(8,128)(2,1)S(1)}, u32[]{:S(2)}, u32[]{:S(2)}) collective-permute-start(bf16[256,256]{1,0:T(8,128)(2,1)S(1)} %dynamic-slice_convert_fusion.5), channel_id=1, source_target_pairs={{0,8},{4,12},{8,0},{12,4},{16,24},{20,28},{24,16},{28,20},{1,9},{5... | collective-permute-start | bytes 393224 | tf_op jit(solution)/shard_map/ppermute | solution.py:50
  183.5 8.8 %collective-permute-start.24 = (bf16[256,128]{1,0:T(8,128)(2,1)S(1)}, bf16[256,128]{1,0:T(8,128)(2,1)S(1)}, u32[]{:S(2)}, u32[]{:S(2)}) collective-permute-start(bf16[256,128]{1,0:T(8,128)(2,1)S(1)} %dynamic-slice_convert_fusion.8), channel_id=1, source_target_pairs={{0,16},{4,20},{8,24},{12,28},{16,0},{20,4},{24,8},{28,12},{1,17},{... | collective-permute-start | bytes 196616 | tf_op jit(solution)/shard_map/ppermute | solution.py:50
  187.5 8.6 %collective-permute-start.15 = (bf16[128,256]{1,0:T(8,128)(2,1)S(1)}, bf16[128,256]{1,0:T(8,128)(2,1)S(1)}, u32[]{:S(2)}, u32[]{:S(2)}) collective-permute-start(bf16[128,256]{1,0:T(8,128)(2,1)S(1)} %dynamic-slice_convert_fusion.11), channel_id=1, source_target_pairs={{0,16},{4,20},{8,24},{12,28},{16,0},{20,4},{24,8},{28,12},{1,17},{... | collective-permute-start | bytes 196616 | tf_op jit(solution)/shard_map/ppermute | solution.py:50
  190.7 7.5 %collective-permute-start.18 = (bf16[128,256]{1,0:T(8,128)(2,1)S(1)}, bf16[128,256]{1,0:T(8,128)(2,1)S(1)}, u32[]{:S(2)}, u32[]{:S(2)}) collective-permute-start(bf16[128,256]{1,0:T(8,128)(2,1)S(1)} %dynamic-slice_convert_fusion.10), channel_id=1, source_target_pairs={{0,16},{4,20},{8,24},{12,28},{16,0},{20,4},{24,8},{28,12},{1,17},{... | collective-permute-start | bytes 196616 | tf_op jit(solution)/shard_map/ppermute | solution.py:50
  192.3 11.8 %collective-permute-start.21 = (bf16[128,256]{1,0:T(8,128)(2,1)S(1)}, bf16[128,256]{1,0:T(8,128)(2,1)S(1)}, u32[]{:S(2)}, u32[]{:S(2)}) collective-permute-start(bf16[128,256]{1,0:T(8,128)(2,1)S(1)} %dynamic-slice_convert_fusion.9), channel_id=1, source_target_pairs={{0,16},{4,20},{8,24},{12,28},{16,0},{20,4},{24,8},{28,12},{1,17},{... | collective-permute-start | bytes 196616 | tf_op jit(solution)/shard_map/ppermute | solution.py:50
  200.1 17.7 %collective-permute-start.29 = (bf16[1024,256]{1,0:T(8,128)(2,1)S(1)}, bf16[1024,256]{1,0:T(8,128)(2,1)S(1)}, u32[]{:S(2)}, u32[]{:S(2)}) collective-permute-start(bf16[1024,256]{1,0:T(8,128)(2,1)S(1)} %dynamic-slice_convert_fusion), channel_id=1, source_target_pairs={{0,8},{4,12},{8,0},{12,4},{16,24},{20,28},{24,16},{28,20},{1,9},{5... | collective-permute-start | bytes 1572872 | tf_op jit(solution)/shard_map/ppermute | solution.py:50
  202.0 27.3 %collective-permute-start.26 = (bf16[256,1024]{1,0:T(8,128)(2,1)S(1)}, bf16[256,1024]{1,0:T(8,128)(2,1)S(1)}, u32[]{:S(2)}, u32[]{:S(2)}) collective-permute-start(bf16[256,1024]{1,0:T(8,128)(2,1)S(1)} %dynamic-slice_convert_fusion.1), channel_id=1, source_target_pairs={{0,8},{4,12},{8,0},{12,4},{16,24},{20,28},{24,16},{28,20},{1,9},{5... | collective-permute-start | bytes 1572872 | tf_op jit(solution)/shard_map/ppermute | solution.py:50
  218.1 18.4 %collective-permute-start.30 = (bf16[1024,128]{1,0:T(8,128)(2,1)S(1)}, bf16[1024,128]{1,0:T(8,128)(2,1)S(1)}, u32[]{:S(2)}, u32[]{:S(2)}) collective-permute-start(bf16[1024,128]{1,0:T(8,128)(2,1)S(1)} %dynamic-slice_convert_fusion.2), channel_id=1, source_target_pairs={{0,16},{4,20},{8,24},{12,28},{16,0},{20,4},{24,8},{28,12},{1,17},{... | collective-permute-start | bytes 786440 | tf_op jit(solution)/shard_map/ppermute | solution.py:50
  229.5 12.1 %collective-permute-start.27 = (bf16[128,1024]{1,0:T(8,128)(2,1)S(1)}, bf16[128,1024]{1,0:T(8,128)(2,1)S(1)}, u32[]{:S(2)}, u32[]{:S(2)}) collective-permute-start(bf16[128,1024]{1,0:T(8,128)(2,1)S(1)} %dynamic-slice_convert_fusion.3), channel_id=1, source_target_pairs={{0,16},{4,20},{8,24},{12,28},{16,0},{20,4},{24,8},{28,12},{1,17},{... | collective-permute-start | bytes 786440 | tf_op jit(solution)/shard_map/ppermute | solution.py:50
  (40 other events, 251.6 us)

commit v2 on v1

--- a/solution.py
+++ b/solution.py
@@ -64,29 +64,99 @@
 
 
 def reverse_blocks(value):
-    bits = axis_bits("dp")
-    rows, width = value.shape
-    split = value.reshape(rows, *([2] * bits), width >> bits)
-    order = (0, *range(bits, 0, -1), bits + 1)
-    return split.transpose(order).reshape(rows, width)
-
-
-def scatter_sum(compute, value, axis):
+    order = [0]
+    for _ in range(axis_bits("dp")):
+        order = [2 * place for place in order] + [2 * place + 1 for place in order]
+    width = value.shape[1] // len(order)
+    return jnp.concatenate(
+        [value[:, place * width : (place + 1) * width] for place in order], axis=1
+    )
+
+
+def scatter_sum(left, right):
     index = lax.axis_index("dp")
-    width = value.shape[1] // 2
+    width = left.shape[1] // 2
     bit = index & 1
-    sent = compute(lax.dynamic_slice_in_dim(value, (1 - bit) * width, width, 1))
+    sent = matmul_tn(lax.dynamic_slice_in_dim(left, (1 - bit) * width, width, 1), right)
     received = swap(sent.astype(jnp.bfloat16), "dp", 0)
-    total = compute(lax.dynamic_slice_in_dim(value, bit * width, width, 1))
+    total = matmul_tn(lax.dynamic_slice_in_dim(left, bit * width, width, 1), right)
     total = total + received.astype(jnp.float32)
     for step in range(1, axis_bits("dp")):
         width //= 2
         bit = (index >> step) & 1
-        sent = lax.dynamic_slice_in_dim(total, (1 - bit) * width, width, axis)
+        sent = lax.dynamic_slice_in_dim(total, (1 - bit) * width, width, 0)
         received = swap(sent.astype(jnp.bfloat16), "dp", step)
-        total = lax.dynamic_slice_in_dim(total, bit * width, width, axis)
+        total = lax.dynamic_slice_in_dim(total, bit * width, width, 0)
         total = total + received.astype(jnp.float32)
     return total
+
+
+def gather_rows(value):
+    for step in reversed(range(axis_bits("dp"))):
+        value = jnp.concatenate([value, swap(value, "dp", step)], axis=0)
+    return value
+
+
+def gather_columns(value):
+    index = lax.axis_index("dp")
+    width = value.shape[-1]
+    for step in reversed(range(axis_bits("dp"))):
+        width //= 2
+        bit = (index >> step) & 1
+        sent = lax.dynamic_slice_in_dim(value, (1 - bit) * width, width, value.ndim - 1)
+        kept = lax.dynamic_slice_in_dim(value, bit * width, width, value.ndim - 1)
+        value = jnp.concatenate([kept, swap(sent, "dp", step)], axis=-2)
+    return value
+
+
+def cut_heads(value, pairs):
+    rows = value.shape[0] // pairs
+    groups = value.shape[1] // (2 * HEAD)
+    return jnp.stack(
+        [
+            value[p * rows : (p + 1) * rows, g * 2 * HEAD : (g + 1) * 2 * HEAD]
+            for p in range(pairs)
+            for g in range(groups)
+        ]
+    )
+
+
+def join_heads(value, pairs):
+    groups = value.shape[0] // pairs
+    return jnp.concatenate(
+        [
+            jnp.concatenate([value[p * groups + g] for g in range(groups)], axis=1)
+            for p in range(pairs)
+        ],
+        axis=0,
+    )
+
+
+def own_head():
+    lane = jnp.arange(2 * HEAD)[None, None, :] // HEAD
+    return lane == 0, lane == 1
+
+
+def spread_heads(value):
+    first, second = own_head()
+    return jnp.concatenate([jnp.where(first, value, 0), jnp.where(second, value, 0)], axis=1)
+
+
+def fold_heads(value):
+    rows = value.shape[1] // 2
+    return jnp.where(own_head()[0], value[:, :rows], value[:, rows:])
+
+
+def batch_nn(left, right):
+    return jnp.einsum("bij,bjk->bik", left, right, preferred_element_type=jnp.float32)
+
+
+def batch_nt(left, right):
+    return jnp.einsum("bij,bkj->bik", left, right, preferred_element_type=jnp.float32)
+
+
+def batch_tn(left, right):
+    return jnp.einsum("bji,bjk->bik", left, right, preferred_element_type=jnp.float32)
 
 
 def masked_max(values, member):
@@ -117,7 +187,7 @@
     pairs_dev, seq_len, model_width = states.shape
     mask_count = positions.shape[1]
     slots = pairs_dev * mask_count
-    heads = proj_weight.shape[2] // HEAD
+    head_width = proj_weight.shape[2]
     flat_rows = states.reshape(pairs_dev * seq_len, model_width)
 
     place_hot = (positions[:, :, None] == jnp.arange(seq_len)[None, None, :]).astype(jnp.bfloat16)
@@ -126,24 +196,22 @@
     ).astype(jnp.bfloat16).reshape(slots, model_width)
 
     query = matmul(picked_states, proj_weight[0]).astype(jnp.bfloat16)
-    query = query.reshape(pairs_dev, mask_count, heads, HEAD)
-    key = matmul(flat_rows, proj_weight[1]).astype(jnp.bfloat16)
-    key = key.reshape(pairs_dev, seq_len, heads, HEAD)
-    val = matmul(flat_rows, proj_weight[2]).astype(jnp.bfloat16)
-    val = val.reshape(pairs_dev, seq_len, heads, HEAD)
-    scores = jnp.einsum(
-        "pqhd,pkhd->phqk", query, key, preferred_element_type=jnp.float32
-    ) * HEAD ** (-0.5)
+    key = cut_heads(matmul(flat_rows, proj_weight[1]).astype(jnp.bfloat16), pairs_dev)
+    val = cut_heads(matmul(flat_rows, proj_weight[2]).astype(jnp.bfloat16), pairs_dev)
+    query = spread_heads(cut_heads(query, pairs_dev))
+    scores = batch_nt(query, key) * HEAD ** (-0.5)
     weights = jnp.exp(scores - jnp.max(scores, axis=-1, keepdims=True))
     soft = weights / jnp.sum(weights, axis=-1, keepdims=True)
     probs = soft.astype(jnp.bfloat16)
-    context = jnp.einsum("phqk,pkhd->pqhd", probs, val, preferred_element_type=jnp.float32)
-    context = context.reshape(slots, heads * HEAD).astype(jnp.bfloat16)
+    context = fold_heads(batch_nn(probs, val)).astype(jnp.bfloat16)
+    context = join_heads(context, pairs_dev)
 
     pre_one = picked_states.astype(jnp.float32) + sum_over_mp(matmul(context, out_weight))
     first_norm = layer_norm(pre_one).astype(jnp.bfloat16)
     inner_act = matmul(first_norm, up_weight)
     activated = gelu_tanh(inner_act).astype(jnp.bfloat16)
+    lefts = gather_rows(jnp.concatenate([activated, context], axis=1))
+    rights = gather_columns(jnp.stack([first_norm, picked_states]))
     pre_two = first_norm.astype(jnp.float32) + sum_over_mp(matmul(activated, down_weight))
     picked = layer_norm(pre_two).astype(jnp.bfloat16)
 
@@ -185,33 +253,32 @@
     dpicked = dpicked * (jnp.repeat(posterior, mask_count)[:, None] / mask_count)
 
     dpre_two = norm_back(pre_two, dpicked).astype(jnp.bfloat16)
-    down_grad = scatter_sum(
-        lambda part: matmul_tn(activated, part), reverse_blocks(dpre_two), 1
-    )
     dinner = gelu_back(inner_act, matmul_nt(dpre_two, down_weight)).astype(jnp.bfloat16)
-    up_grad = scatter_sum(lambda part: matmul_tn(part, dinner), reverse_blocks(first_norm), 0)
+    dinner_all = gather_rows(dinner)
     dfirst = dpre_two.astype(jnp.float32) + sum_over_mp(matmul_nt(dinner, up_weight))
     dpre_one = norm_back(pre_one, dfirst).astype(jnp.bfloat16)
-    out_grad = scatter_sum(lambda part: matmul_tn(context, part), reverse_blocks(dpre_one), 1)
+    dpre = gather_columns(jnp.stack([dpre_two, dpre_one]))
 
     dcontext = matmul_nt(dpre_one, out_weight).astype(jnp.bfloat16)
-    dcontext = dcontext.reshape(pairs_dev, mask_count, heads, HEAD)
-    turned = reverse_blocks(flat_rows)
-    dval = jnp.einsum("phqk,pqhd->pkhd", probs, dcontext, preferred_element_type=jnp.float32)
-    dval = dval.astype(jnp.bfloat16).reshape(pairs_dev * seq_len, heads * HEAD)
-    val_grad = scatter_sum(lambda part: matmul_tn(part, dval), turned, 0)
-    dprobs = jnp.einsum("pqhd,pkhd->phqk", dcontext, val, preferred_element_type=jnp.float32)
+    dcontext = spread_heads(cut_heads(dcontext, pairs_dev))
+    dval = batch_tn(probs, dcontext).astype(jnp.bfloat16)
+    dprobs = batch_nt(dcontext, val)
     dscores = soft * (dprobs - jnp.sum(soft * dprobs, axis=-1, keepdims=True))
     dscores = (dscores * HEAD ** (-0.5)).astype(jnp.bfloat16)
-    dkey = jnp.einsum("phqk,pqhd->pkhd", dscores, query, preferred_element_type=jnp.float32)
-    dkey = dkey.astype(jnp.bfloat16).reshape(pairs_dev * seq_len, heads * HEAD)
-    key_grad = scatter_sum(lambda part: matmul_tn(part, dkey), turned, 0)
-    dquery = jnp.einsum("phqk,pkhd->pqhd", dscores, key, preferred_element_type=jnp.float32)
-    dquery = dquery.astype(jnp.bfloat16).reshape(slots, heads * HEAD)
-    query_grad = scatter_sum(
-        lambda part: matmul_tn(part, dquery), reverse_blocks(picked_states), 0
-    )
-    proj_grad = jnp.stack([query_grad, key_grad, val_grad])
+    dkey = batch_tn(dscores, query).astype(jnp.bfloat16)
+    dquery = join_heads(fold_heads(batch_nn(dscores, key)).astype(jnp.bfloat16), pairs_dev)
+    dquery_all = gather_rows(dquery)
+    dkey_val = jnp.concatenate([join_heads(dkey, pairs_dev), join_heads(dval, pairs_dev)], axis=1)
+    key_val_grad = scatter_sum(reverse_blocks(flat_rows), dkey_val)
+
+    ff_width = activated.shape[1]
+    down_grad = matmul_tn(lefts[:, :ff_width], dpre[0])
+    out_grad = matmul_tn(lefts[:, ff_width:], dpre[1])
+    up_grad = matmul_tn(rights[0], dinner_all)
+    query_grad = matmul_tn(rights[1], dquery_all)
+    proj_grad = jnp.stack(
+        [query_grad, key_val_grad[:, :head_width], key_val_grad[:, head_width:]]
+    )
     return (proj_grad, out_grad, up_grad, down_grad, score_grad)
 
 

time: 243 us -> 220 us (0.905)
  waiting for transfers between devices: 99.9 us -> 86.5 us
  local copies, waits for them, and re-layouts: 37.9 us -> 26.2 us
  other arithmetic: 12.2 us -> 21.4 us
  matrix products: 53.4 us -> 47.2 us
    reshape x15 -> x0, local copies, waits for them, and re-layouts: 14.9 us -> none  [the longest x6 6.75 us: reverse_blocks(): split = value.reshape(rows, *[2] * bits, width >> bits)]
    ppermute x31, waiting for transfers between devices: 99.9 us -> 86.5 us  [swap(): return lax.ppermute(value, axis, pairs)]
    unnamed x84 -> x131, local copies, waits for them, and re-layouts: 4.36 us -> 11 us
    concatenate x0 -> x12, other arithmetic: none -> 6.35 us  [the longest x6 5.2 us: gather_rows(): value = jnp.concatenate([value, swap(value, 'dp', step)], axis=0)]
    transpose x1 -> x0, local copies, waits for them, and re-layouts: 6.21 us -> none  [reverse_blocks(): return split.transpose(order).reshape(rows, width)]
    another operation x3 -> x5, local copies, waits for them, and re-layouts: 5.51 us -> 0.23 us  [the longest x4 0.21 us: cut_heads(): jnp.stack([value[p * rows:(p + 1) * rows, g * 2 * HEAD:(g + 1) * 2 * HEAD...]
    convert_element_type x5 -> x0, local copies, waits for them, and re-layouts: 4.33 us -> none  [the longest x1 1.58 us: local(): dkey = dkey.astype(jnp.bfloat16).reshape(pairs_dev * seq_len, heads * HEAD)]
    add x9 -> x2, other arithmetic: 2.81 us -> 0.1 us  [scatter_sum(): total = total + received.astype(jnp.float32)]
  transfers between devices with their start and end apart: 31 -> 31, of which waited for: 22 -> 12; matrix products, arithmetic and copies ran while one was open for 26% -> 34% of each run, Pallas kernels for 0% -> 0%
where the time goes in v2:
time: 220 us; the launch traced here: 219 us
  waiting for transfers between devices  86.5 us (39%)
  matrix products  47.2 us (21%)
  starting transfers between devices  35.8 us (16%)
  local copies, waits for them, and re-layouts  26.2 us (12%)
  other arithmetic  21.4 us (10%)
    ppermute x31, waiting for transfers between devices, swap(): return lax.ppermute(value, axis, pairs)  86.5 us
    ppermute x31, starting transfers between devices, swap(): return lax.ppermute(value, axis, pairs)  35.8 us
    dot_general x7, matrix products, matmul(): return jnp.dot(left, right, preferred_element_type=jnp.float32)  11.7 us
    unnamed x131, local copies, waits for them, and re-layouts  11 us
    dot_general x6, matrix products, matmul_tn(): lax.dot_general(left, right, (((0,), (0,)), ((), ())), preferred_element_...  9.99 us
    dot_general x4, matrix products, matmul_nt(): lax.dot_general(left, right, (((1,), (1,)), ((), ())), preferred_element_...  8.59 us
    dot_general x2, matrix products, batch_nn(): jnp.einsum('bij,bjk->bik', left, right, preferred_element_type=jnp.float32)  7.42 us
    dot_general x2, matrix products, batch_tn(): jnp.einsum('bji,bjk->bik', left, right, preferred_element_type=jnp.float32)  6.26 us
  transfers between devices with their start and end apart: 31, of which 12 were waited for; matrix products, arithmetic and copies ran while one was open for 34% of the time, Pallas kernels for 0%

profile of v2, /device:TPU:0, one launch (start us, length us, event | category | flops | bytes accessed | tf_op | source)
XLA Modules:
  0.0 218.8 jit_solution(800395329527646481)
XLA Ops:
  0.7 2.5 %convolution_convert_fusion.2 = bf16[1024,256]{1,0:T(8,128)(2,1)S(1)} fusion(bf16[1024,1024]{1,0:T(8,128)(2,1)} %bitcast.256, bf16[3,1024,256]{2,1,0:T(8,128)(2,1)} %param.15), kind=kOutput, calls=%fused_computation.33 | convolution fusion | flops 537133056 | bytes 3145728 | tf_op jit(solution)/shard_map/dot_general | solution.py:10
  7.4 1.7 fusion.93
  11.9 1.7 slice_dynamic-update-slice_fusion.2
  13.7 2.6 %collective-permute-start.1 = (bf16[128,1024]{1,0:T(8,128)(2,1)S(1)}, bf16[128,1024]{1,0:T(8,128)(2,1)S(1)}, u32[]{:S(2)}, u32[]{:S(2)}) collective-permute-start(bf16[128,1024]{1,0:T(8,128)(2,1)S(1)} %add_convert_fusion.5), channel_id=1, source_target_pairs={{0,2},{1,3},{2,0},{3,1},{4,6},{5,7},{6,4},{7,5},{8,10},{9,11},{10,... | collective-permute-start | bytes 786440 | tf_op jit(solution)/shard_map/ppermute | solution.py:50
  19.2 4.1 %collective-permute-done.1 = bf16[128,1024]{1,0:T(8,128)(2,1)S(1)} collective-permute-done((bf16[128,1024]{1,0:T(8,128)(2,1)S(1)}, bf16[128,1024]{1,0:T(8,128)(2,1)S(1)}, u32[]{:S(2)}, u32[]{:S(2)}) %collective-permute-start.1) | collective-permute-done | bytes 262176 | tf_op jit(solution)/shard_map/ppermute | solution.py:50
  25.8 1.7 slice_dynamic-update-slice_fusion
  27.6 2.9 %collective-permute-start.2 = (bf16[2,128,512]{2,1,0:T(8,128)(2,1)S(1)}, bf16[2,128,512]{2,1,0:T(8,128)(2,1)S(1)}, u32[]{:S(2)}, u32[]{:S(2)}) collective-permute-start(bf16[2,128,512]{2,1,0:T(8,128)(2,1)S(1)} %get-tuple-element.37), channel_id=1, source_target_pairs={{0,16},{4,20},{8,24},{12,28},{16,0},{20,4},{24,8},{28,12},{1,17},{... | collective-permute-start | bytes 786440 | tf_op jit(solution)/shard_map/ppermute | solution.py:50
  32.5 17.8 %collective-permute-done.2 = bf16[2,128,512]{2,1,0:T(8,128)(2,1)S(1)} collective-permute-done((bf16[2,128,512]{2,1,0:T(8,128)(2,1)S(1)}, bf16[2,128,512]{2,1,0:T(8,128)(2,1)S(1)}, u32[]{:S(2)}, u32[]{:S(2)}) %collective-permute-start.2) | collective-permute-done | bytes 262176 | tf_op jit(solution)/shard_map/ppermute | solution.py:50
  52.0 6.4 %fusion.161 = (f32[128]{0:T(128)S(1)}, f32[128,4096]{1,0:T(8,128)S(1)}) fusion(bf16[4096,1024]{1,0:T(8,128)(2,1)} %param.19, f32[128]{0:T(128)S(1)} %fusion.138, f32[128]{0:T(128)S(1)} %broadcast_multiply_fusion.1, bf16[128,1024]{1,0:T(8,128)(2,1)S(1)} %collective-permute-done.6, bf16[128,1024]{1,0:T(8,128)(2,1)S(1)} %add_convert_fusion.4, ...), kind=kOutput, calls=%fused_computation.370 | convolution fusion | flops 1075314560 | bytes 11273728 | tf_op jit(solution)/shard_map/dot_general | solution.py:20
  75.6 6.3 %convolution_convert_fusion.6 = bf16[128,1024]{1,0:T(8,128)(2,1)} fusion(bf16[4096,1024]{1,0:T(8,128)(2,1)} %param.19, f32[128,4096]{1,0:T(8,128)} %copy-done.3, f32[128]{0:T(128)S(1)} %get-tuple-element.25, f32[128]{0:T(128)S(1)} %get-tuple-element.26, s32[128]{0:T(128)} %sub.269), kind=kOutput, calls=%fused_computation.38 | convolution fusion | flops 1077018624 | bytes 10749440 | tf_op jit(solution)/shard_map/dot_general | solution.py:10
  89.5 3.1 %collective-permute-done.11 = f32[2,2,2]{2,1,0:T(2,128)S(1)} collective-permute-done((f32[2,2,2]{2,1,0:T(2,128)S(1)}, f32[2,2,2]{2,1,0:T(2,128)S(1)}, u32[]{:S(2)}, u32[]{:S(2)}) %collective-permute-start.11) | collective-permute-done | bytes 64 | tf_op jit(solution)/shard_map/ppermute | solution.py:50
  93.0 3.3 %collective-permute-done.12 = f32[2,2,2]{2,1,0:T(2,128)S(1)} collective-permute-done((f32[2,2,2]{2,1,0:T(2,128)S(1)}, f32[2,2,2]{2,1,0:T(2,128)S(1)}, u32[]{:S(2)}, u32[]{:S(2)}) %collective-permute-start.12) | collective-permute-done | bytes 64 | tf_op jit(solution)/shard_map/ppermute | solution.py:50
  96.3 1.9 collective-permute-start.13
  98.2 2.7 %collective-permute-done.13 = f32[2,2,2]{2,1,0:T(2,128)S(1)} collective-permute-done((f32[2,2,2]{2,1,0:T(2,128)S(1)}, f32[2,2,2]{2,1,0:T(2,128)S(1)}, u32[]{:S(2)}, u32[]{:S(2)}) %collective-permute-start.13) | collective-permute-done | bytes 64 | tf_op jit(solution)/shard_map/ppermute | solution.py:50
  100.9 1.8 add_convert_fusion.3
  104.7 4.7 %collective-permute-done.10 = bf16[128,1024]{1,0:T(8,128)(2,1)} collective-permute-done((bf16[128,1024]{1,0:T(8,128)(2,1)}, bf16[128,1024]{1,0:T(8,128)(2,1)}, u32[]{:S(2)}, u32[]{:S(2)}) %collective-permute-start.10) | collective-permute-done | bytes 262176 | tf_op jit(solution)/shard_map/ppermute | solution.py:50
  115.1 2.3 %pad_maximum_fusion.11 = bf16[512,1280]{1,0:T(8,128)(2,1)} fusion(bf16[256,1280]{1,0:T(8,128)(2,1)} %collective-permute-done.23, bf16[128,1280]{1,0:T(8,128)(2,1)S(1)} %copy-done.15, bf16[64,128]{1,0:T(8,128)(2,1)S(1)} %get-tuple-element.68, bf16[64,128]{1,0:T(8,128)(2,1)S(1)} %get-tuple-element.69, bf16[64,128]{1,0:T(8,128)(2,1)S(1)} %get-tuple-element.70, ...), kind=kLoop, calls=%fused_computation.30 | loop fusion | flops 9175040 | bytes 2621440 | tf_op jit(solution)/shard_map/concatenate | solution.py:96
  118.0 1.8 collective-permute-start.28
  121.3 11.5 %collective-permute-done.28 = bf16[128,1024]{1,0:T(8,128)(2,1)S(1)} collective-permute-done((bf16[128,1024]{1,0:T(8,128)(2,1)S(1)}, bf16[128,1024]{1,0:T(8,128)(2,1)S(1)}, u32[]{:S(2)}, u32[]{:S(2)}) %collective-permute-start.28) | collective-permute-done | bytes 262176 | tf_op jit(solution)/shard_map/ppermute | solution.py:50
  138.0 5.9 %convolution_convert_fusion.1 = bf16[4,512,128]{1,2,0:T(8,128)(2,1)} fusion(f32[4,128,512]{2,1,0:T(8,128)} %fusion.98, bf16[4,64,128]{2,1,0:T(8,128)(2,1)} %copy-done.35, bf16[4,64,128]{2,1,0:T(8,128)(2,1)S(1)} %get-tuple-element.71, f32[4,128,512]{2,1,0:T(8,128)} %get-tuple-element.89, f32[4,128]{1,0:T(4,128)S(1)} %copy-done.60), kind=kOutput, calls=%fused_computation.32 | convolution fusion | flops 69469184 | bytes 2754560 | tf_op jit(solution)/shard_map/bji,bjk->bik/dot_general | solution.py:159
  143.9 5.7 %fusion.29 = bf16[4,128,128]{2,1,0:T(8,128)(2,1)} fusion(f32[4,128,512]{2,1,0:T(8,128)} %fusion.98, bf16[1,512,128]{2,1,0:T(8,128)(2,1)} %copy-done.24, bf16[1,512,128]{2,1,0:T(8,128)(2,1)} %copy-done.25, bf16[1,512,128]{2,1,0:T(8,128)(2,1)} %copy-done.26, bf16[1,512,128]{2,1,0:T(8,128)(2,1)} %copy-done.23, f32[4,128,512]{2,1,0:T(8,128)} %get-tuple-element.89, ...), kind=kOutput, calls=%fused_computation.54 | convolution fusion | flops 69731328 | bytes 2754560 | tf_op jit(solution)/shard_map/bij,bjk->bik/dot_general | solution.py:151
  150.8 3.2 %collective-permute-start.16 = (bf16[128,256]{1,0:T(8,128)(2,1)S(1)}, bf16[128,256]{1,0:T(8,128)(2,1)S(1)}, u32[]{:S(2)}, u32[]{:S(2)}) collective-permute-start(bf16[128,256]{1,0:T(8,128)(2,1)S(1)} %maximum_maximum_fusion.2), channel_id=1, source_target_pairs={{0,16},{4,20},{8,24},{12,28},{16,0},{20,4},{24,8},{28,12},{1,17},{... | collective-permute-start | bytes 196616 | tf_op jit(solution)/shard_map/ppermute | solution.py:50
  154.9 1.8 collective-permute-done.16
  156.7 6.6 %collective-permute-start.17 = (bf16[256,256]{1,0:T(8,128)(2,1)S(1)}, bf16[256,256]{1,0:T(8,128)(2,1)S(1)}, u32[]{:S(2)}, u32[]{:S(2)}) collective-permute-start(bf16[256,256]{1,0:T(8,128)(2,1)S(1)} %pad_maximum_fusion.23), channel_id=1, source_target_pairs={{0,8},{4,12},{8,0},{12,4},{16,24},{20,28},{24,16},{28,20},{1,9},{5... | collective-permute-start | bytes 393224 | tf_op jit(solution)/shard_map/ppermute | solution.py:50
  163.3 6.7 %collective-permute-done.17 = bf16[256,256]{1,0:T(8,128)(2,1)S(1)} collective-permute-done((bf16[256,256]{1,0:T(8,128)(2,1)S(1)}, bf16[256,256]{1,0:T(8,128)(2,1)S(1)}, u32[]{:S(2)}, u32[]{:S(2)}) %collective-permute-start.17) | collective-permute-done | bytes 131104 | tf_op jit(solution)/shard_map/ppermute | solution.py:50
  173.4 14.3 %collective-permute-done.18 = bf16[512,256]{1,0:T(8,128)(2,1)S(1)} collective-permute-done((bf16[512,256]{1,0:T(8,128)(2,1)S(1)}, bf16[512,256]{1,0:T(8,128)(2,1)S(1)}, u32[]{:S(2)}, u32[]{:S(2)}) %collective-permute-start.18) | collective-permute-done | bytes 262176 | tf_op jit(solution)/shard_map/ppermute | solution.py:50
  192.1 4.4 %collective-permute-done.20 = bf16[256,512]{1,0:T(8,128)(2,1)S(1)} collective-permute-done((bf16[256,512]{1,0:T(8,128)(2,1)S(1)}, bf16[256,512]{1,0:T(8,128)(2,1)S(1)}, u32[]{:S(2)}, u32[]{:S(2)}) %collective-permute-start.20) | collective-permute-done | bytes 262176 | tf_op jit(solution)/shard_map/ppermute | solution.py:50
  196.6 1.8 collective-permute-start.21
  198.4 12.3 %collective-permute-done.27 = bf16[2,512,128]{2,1,0:T(8,128)(2,1)S(1)} collective-permute-done((bf16[2,512,128]{2,1,0:T(8,128)(2,1)S(1)}, bf16[2,512,128]{2,1,0:T(8,128)(2,1)S(1)}, u32[]{:S(2)}, u32[]{:S(2)}) %collective-permute-start.27) | collective-permute-done | bytes 262176 | tf_op jit(solution)/shard_map/ppermute | solution.py:50
  210.6 2.9 %fusion.2 = f32[1024,128]{1,0:T(8,128)} fusion(bf16[512,1280]{1,0:T(8,128)(2,1)} %collective-permute-done.24, bf16[256,1280]{1,0:T(8,128)(2,1)} %collective-permute-done.23, bf16[128,1280]{1,0:T(8,128)(2,1)S(1)} %copy-done.16, bf16[128,1024]{1,0:T(8,128)(2,1)S(1)} %copy-done.7, bf16[64,128]{1,0:T(8,128)(2,1)S(1)} %get-tuple-element.68, ...), kind=kOutput, calls=%fused_computation.3 | convolution fusion | flops 285736960 | bytes 3670016 | tf_op jit(solution)/shard_map/dot_general | solution.py:14
  213.6 2.0 fusion.41
  216.4 2.4 %fusion.7 = f32[128,1024]{1,0:T(8,128)} fusion(bf16[512,1024]{1,0:T(8,128)(2,1)S(1)} %collective-permute-done.30, bf16[256,1024]{1,0:T(8,128)(2,1)} %collective-permute-done.29, bf16[128,1024]{1,0:T(8,128)(2,1)S(1)} %copy-done.20, bf16[128,1024]{1,0:T(8,128)(2,1)S(1)} %copy-done.9, bf16[2,512,128]{2,1,0:T(8,128)(2,1)} %collective-permute-done.4, ...), kind=kOutput, calls=%fused_computation.12 | convolution fusion | flops 277348352 | bytes 3145728 | tf_op jit(solution)/shard_map/dot_general | solution.py:14
  (280 shorter events, 66.5 us)
Async XLA Ops:
  9.5 4.2 %collective-permute-start = (bf16[128,1024]{1,0:T(8,128)(2,1)S(1)}, bf16[128,1024]{1,0:T(8,128)(2,1)S(1)}, u32[]{:S(2)}, u32[]{:S(2)}) collective-permute-start(bf16[128,1024]{1,0:T(8,128)(2,1)S(1)} %convolution_convert_fusion.8), channel_id=1, source_target_pairs={{0,1},{1,0},{2,3},{3,2},{4,5},{5,4},{6,7},{7,6},{8,9},{9,8},{10,11... | collective-permute-start | bytes 786440 | tf_op jit(solution)/shard_map/ppermute | solution.py:50
  13.7 9.5 %collective-permute-start.1 = (bf16[128,1024]{1,0:T(8,128)(2,1)S(1)}, bf16[128,1024]{1,0:T(8,128)(2,1)S(1)}, u32[]{:S(2)}, u32[]{:S(2)}) collective-permute-start(bf16[128,1024]{1,0:T(8,128)(2,1)S(1)} %add_convert_fusion.5), channel_id=1, source_target_pairs={{0,2},{1,3},{2,0},{3,1},{4,6},{5,7},{6,4},{7,5},{8,10},{9,11},{10,... | collective-permute-start | bytes 786440 | tf_op jit(solution)/shard_map/ppermute | solution.py:50
  25.1 35.4 %copy-start.6 = (bf16[128,1024]{1,0:T(8,128)(2,1)}, bf16[128,1024]{1,0:T(8,128)(2,1)S(1)}, u32[]{:S(2)}) copy-start(bf16[128,1024]{1,0:T(8,128)(2,1)S(1)} %get-tuple-element.90) | copy-start | bytes 786436
  25.8 4.7 %collective-permute-start.5 = (bf16[128,1024]{1,0:T(8,128)(2,1)S(1)}, bf16[128,1024]{1,0:T(8,128)(2,1)S(1)}, u32[]{:S(2)}, u32[]{:S(2)}) collective-permute-start(bf16[128,1024]{1,0:T(8,128)(2,1)S(1)} %convolution_convert_fusion.7), channel_id=1, source_target_pairs={{0,1},{1,0},{2,3},{3,2},{4,5},{5,4},{6,7},{7,6},{8,9},{9,8},{10,11... | collective-permute-start | bytes 786440 | tf_op jit(solution)/shard_map/ppermute | solution.py:50
  27.6 22.8 %collective-permute-start.2 = (bf16[2,128,512]{2,1,0:T(8,128)(2,1)S(1)}, bf16[2,128,512]{2,1,0:T(8,128)(2,1)S(1)}, u32[]{:S(2)}, u32[]{:S(2)}) collective-permute-start(bf16[2,128,512]{2,1,0:T(8,128)(2,1)S(1)} %get-tuple-element.37), channel_id=1, source_target_pairs={{0,16},{4,20},{8,24},{12,28},{16,0},{20,4},{24,8},{28,12},{1,17},{... | collective-permute-start | bytes 786440 | tf_op jit(solution)/shard_map/ppermute | solution.py:50
  30.5 20.4 %collective-permute-start.6 = (bf16[128,1024]{1,0:T(8,128)(2,1)S(1)}, bf16[128,1024]{1,0:T(8,128)(2,1)S(1)}, u32[]{:S(2)}, u32[]{:S(2)}) collective-permute-start(bf16[128,1024]{1,0:T(8,128)(2,1)S(1)} %add_convert_fusion.4), channel_id=1, source_target_pairs={{0,2},{1,3},{2,0},{3,1},{4,6},{5,7},{6,4},{7,5},{8,10},{9,11},{10,... | collective-permute-start | bytes 786440 | tf_op jit(solution)/shard_map/ppermute | solution.py:50
  32.1 28.4 %collective-permute-start.22 = (bf16[128,1280]{1,0:T(8,128)(2,1)S(1)}, bf16[128,1280]{1,0:T(8,128)(2,1)S(1)}, u32[]{:S(2)}, u32[]{:S(2)}) collective-permute-start(bf16[128,1280]{1,0:T(8,128)(2,1)S(1)} %maximum_maximum_fusion.1), channel_id=1, source_target_pairs={{0,16},{4,20},{8,24},{12,28},{16,0},{20,4},{24,8},{28,12},{1,17},{... | collective-permute-start | bytes 983048 | tf_op jit(solution)/shard_map/ppermute | solution.py:50
  50.4 15.5 %collective-permute-start.3 = (bf16[2,256,256]{2,1,0:T(8,128)(2,1)S(1)}, bf16[2,256,256]{2,1,0:T(8,128)(2,1)S(1)}, u32[]{:S(2)}, u32[]{:S(2)}) collective-permute-start(bf16[2,256,256]{2,1,0:T(8,128)(2,1)S(1)} %get-tuple-element.35), channel_id=1, source_target_pairs={{0,8},{4,12},{8,0},{12,4},{16,24},{20,28},{24,16},{28,20},{1,9},{5... | collective-permute-start | bytes 786440 | tf_op jit(solution)/shard_map/ppermute | solution.py:50
  60.5 2.6 %collective-permute-start.7 = (f32[3,128]{1,0:T(4,128)S(1)}, f32[3,128]{1,0:T(4,128)S(1)}, u32[]{:S(2)}, u32[]{:S(2)}) collective-permute-start(f32[3,128]{1,0:T(4,128)S(1)} %pad_maximum_fusion.42), channel_id=1, source_target_pairs={{0,1},{1,0},{2,3},{3,2},{4,5},{5,4},{6,7},{7,6},{8,9},{9,8},{10,11... | collective-permute-start | bytes 4616 | tf_op jit(solution)/shard_map/ppermute | solution.py:50
  61.5 53.5 %collective-permute-start.23 = (bf16[256,1280]{1,0:T(8,128)(2,1)}, bf16[256,1280]{1,0:T(8,128)(2,1)}, u32[]{:S(2)}, u32[]{:S(2)}) collective-permute-start(bf16[256,1280]{1,0:T(8,128)(2,1)} %pad_maximum_fusion.13), channel_id=1, source_target_pairs={{0,8},{4,12},{8,0},{12,4},{16,24},{20,28},{24,16},{28,20},{1,9},{5... | collective-permute-start | bytes 1966088 | tf_op jit(solution)/shard_map/ppermute | solution.py:50
  64.3 10.5 %collective-permute-start.8 = (f32[3,128]{1,0:T(4,128)}, f32[3,128]{1,0:T(4,128)}, u32[]{:S(2)}, u32[]{:S(2)}) collective-permute-start(f32[3,128]{1,0:T(4,128)} %pad_maximum_fusion.43), channel_id=1, source_target_pairs={{0,2},{1,3},{2,0},{3,1},{4,6},{5,7},{6,4},{7,5},{8,10},{9,11},{10,... | collective-permute-start | bytes 4616 | tf_op jit(solution)/shard_map/ppermute | solution.py:50
  69.4 120.7 %collective-permute-start.4 = (bf16[2,512,128]{2,1,0:T(8,128)(2,1)}, bf16[2,512,128]{2,1,0:T(8,128)(2,1)}, u32[]{:S(2)}, u32[]{:S(2)}) collective-permute-start(bf16[2,512,128]{2,1,0:T(8,128)(2,1)} %get-tuple-element.33), channel_id=1, source_target_pairs={{0,4},{4,0},{8,12},{12,8},{16,20},{20,16},{24,28},{28,24},{1,5},{5... | collective-permute-start | bytes 786440 | tf_op jit(solution)/shard_map/ppermute | solution.py:50
  81.8 19.0 %collective-permute-start.9 = (bf16[128,1024]{1,0:T(8,128)(2,1)}, bf16[128,1024]{1,0:T(8,128)(2,1)}, u32[]{:S(2)}, u32[]{:S(2)}) collective-permute-start(bf16[128,1024]{1,0:T(8,128)(2,1)} %convolution_convert_fusion.6), channel_id=1, source_target_pairs={{0,1},{1,0},{2,3},{3,2},{4,5},{5,4},{6,7},{7,6},{8,9},{9,8},{10,11... | collective-permute-start | bytes 786440 | tf_op jit(solution)/shard_map/ppermute | solution.py:50
  88.9 3.7 %collective-permute-start.11 = (f32[2,2,2]{2,1,0:T(2,128)S(1)}, f32[2,2,2]{2,1,0:T(2,128)S(1)}, u32[]{:S(2)}, u32[]{:S(2)}) collective-permute-start(f32[2,2,2]{2,1,0:T(2,128)S(1)} %pad_maximum_fusion.44), channel_id=1, source_target_pairs={{0,4},{4,0},{8,12},{12,8},{16,20},{20,16},{24,28},{28,24},{1,5},{5... | collective-permute-start | bytes 104 | tf_op jit(solution)/shard_map/ppermute | solution.py:50
  92.6 3.7 %collective-permute-start.12 = (f32[2,2,2]{2,1,0:T(2,128)S(1)}, f32[2,2,2]{2,1,0:T(2,128)S(1)}, u32[]{:S(2)}, u32[]{:S(2)}) collective-permute-start(f32[2,2,2]{2,1,0:T(2,128)S(1)} %pad_maximum_fusion.45), channel_id=1, source_target_pairs={{0,8},{4,12},{8,0},{12,4},{16,24},{20,28},{24,16},{28,20},{1,9},{5... | collective-permute-start | bytes 104 | tf_op jit(solution)/shard_map/ppermute | solution.py:50
  96.3 4.5 %collective-permute-start.13 = (f32[2,2,2]{2,1,0:T(2,128)S(1)}, f32[2,2,2]{2,1,0:T(2,128)S(1)}, u32[]{:S(2)}, u32[]{:S(2)}) collective-permute-start(f32[2,2,2]{2,1,0:T(2,128)S(1)} %pad_maximum_fusion.46), channel_id=1, source_target_pairs={{0,16},{4,20},{8,24},{12,28},{16,0},{20,4},{24,8},{28,12},{1,17},{... | collective-permute-start | bytes 104 | tf_op jit(solution)/shard_map/ppermute | solution.py:50
  102.7 6.7 %collective-permute-start.10 = (bf16[128,1024]{1,0:T(8,128)(2,1)}, bf16[128,1024]{1,0:T(8,128)(2,1)}, u32[]{:S(2)}, u32[]{:S(2)}) collective-permute-start(bf16[128,1024]{1,0:T(8,128)(2,1)} %add_convert_fusion.3), channel_id=1, source_target_pairs={{0,2},{1,3},{2,0},{3,1},{4,6},{5,7},{6,4},{7,5},{8,10},{9,11},{10,... | collective-permute-start | bytes 786440 | tf_op jit(solution)/shard_map/ppermute | solution.py:50
  114.9 4.9 %collective-permute-start.14 = (bf16[128,1024]{1,0:T(8,128)(2,1)S(1)}, bf16[128,1024]{1,0:T(8,128)(2,1)S(1)}, u32[]{:S(2)}, u32[]{:S(2)}) collective-permute-start(bf16[128,1024]{1,0:T(8,128)(2,1)S(1)} %convolution_convert_fusion.5), channel_id=1, source_target_pairs={{0,1},{1,0},{2,3},{3,2},{4,5},{5,4},{6,7},{7,6},{8,9},{9,8},{10,11... | collective-permute-start | bytes 786440 | tf_op jit(solution)/shard_map/ppermute | solution.py:50
  117.4 80.9 %collective-permute-start.24 = (bf16[512,1280]{1,0:T(8,128)(2,1)}, bf16[512,1280]{1,0:T(8,128)(2,1)}, u32[]{:S(2)}, u32[]{:S(2)}) collective-permute-start(bf16[512,1280]{1,0:T(8,128)(2,1)} %pad_maximum_fusion.11), channel_id=1, source_target_pairs={{0,4},{4,0},{8,12},{12,8},{16,20},{20,16},{24,28},{28,24},{1,5},{5... | collective-permute-start | bytes 3932168 | tf_op jit(solution)/shard_map/ppermute | solution.py:50
  118.0 14.8 %collective-permute-start.28 = (bf16[128,1024]{1,0:T(8,128)(2,1)S(1)}, bf16[128,1024]{1,0:T(8,128)(2,1)S(1)}, u32[]{:S(2)}, u32[]{:S(2)}) collective-permute-start(bf16[128,1024]{1,0:T(8,128)(2,1)S(1)} %fusion.40), channel_id=1, source_target_pairs={{0,16},{4,20},{8,24},{12,28},{16,0},{20,4},{24,8},{28,12},{1,17},{... | collective-permute-start | bytes 786440 | tf_op jit(solution)/shard_map/ppermute | solution.py:50
  119.9 14.4 %collective-permute-start.15 = (bf16[128,1024]{1,0:T(8,128)(2,1)S(1)}, bf16[128,1024]{1,0:T(8,128)(2,1)S(1)}, u32[]{:S(2)}, u32[]{:S(2)}) collective-permute-start(bf16[128,1024]{1,0:T(8,128)(2,1)S(1)} %add_convert_fusion.1), channel_id=1, source_target_pairs={{0,2},{1,3},{2,0},{3,1},{4,6},{5,7},{6,4},{7,5},{8,10},{9,11},{10,... | collective-permute-start | bytes 786440 | tf_op jit(solution)/shard_map/ppermute | solution.py:50
  134.3 37.9 %collective-permute-start.29 = (bf16[256,1024]{1,0:T(8,128)(2,1)}, bf16[256,1024]{1,0:T(8,128)(2,1)}, u32[]{:S(2)}, u32[]{:S(2)}) collective-permute-start(bf16[256,1024]{1,0:T(8,128)(2,1)} %pad_maximum_fusion.16), channel_id=1, source_target_pairs={{0,8},{4,12},{8,0},{12,4},{16,24},{20,28},{24,16},{28,20},{1,9},{5... | collective-permute-start | bytes 1572872 | tf_op jit(solution)/shard_map/ppermute | solution.py:50
  150.8 5.9 %collective-permute-start.16 = (bf16[128,256]{1,0:T(8,128)(2,1)S(1)}, bf16[128,256]{1,0:T(8,128)(2,1)S(1)}, u32[]{:S(2)}, u32[]{:S(2)}) collective-permute-start(bf16[128,256]{1,0:T(8,128)(2,1)S(1)} %maximum_maximum_fusion.2), channel_id=1, source_target_pairs={{0,16},{4,20},{8,24},{12,28},{16,0},{20,4},{24,8},{28,12},{1,17},{... | collective-permute-start | bytes 196616 | tf_op jit(solution)/shard_map/ppermute | solution.py:50
  154.0 17.5 %collective-permute-start.25 = (bf16[2,128,512]{2,1,0:T(8,128)(2,1)S(1)}, bf16[2,128,512]{2,1,0:T(8,128)(2,1)S(1)}, u32[]{:S(2)}, u32[]{:S(2)}) collective-permute-start(bf16[2,128,512]{2,1,0:T(8,128)(2,1)S(1)} %get-tuple-element.31), channel_id=1, source_target_pairs={{0,16},{4,20},{8,24},{12,28},{16,0},{20,4},{24,8},{28,12},{1,17},{... | collective-permute-start | bytes 786440 | tf_op jit(solution)/shard_map/ppermute | solution.py:50
  156.7 13.3 %collective-permute-start.17 = (bf16[256,256]{1,0:T(8,128)(2,1)S(1)}, bf16[256,256]{1,0:T(8,128)(2,1)S(1)}, u32[]{:S(2)}, u32[]{:S(2)}) collective-permute-start(bf16[256,256]{1,0:T(8,128)(2,1)S(1)} %pad_maximum_fusion.23), channel_id=1, source_target_pairs={{0,8},{4,12},{8,0},{12,4},{16,24},{20,28},{24,16},{28,20},{1,9},{5... | collective-permute-start | bytes 393224 | tf_op jit(solution)/shard_map/ppermute | solution.py:50
  170.0 19.2 %collective-permute-start.19 = (bf16[512,512]{1,0:T(8,128)(2,1)S(1)}, bf16[512,512]{1,0:T(8,128)(2,1)S(1)}, u32[]{:S(2)}, u32[]{:S(2)}) collective-permute-start(bf16[512,512]{1,0:T(8,128)(2,1)S(1)} %convolution_convert_fusion.4), channel_id=1, source_target_pairs={{0,4},{4,0},{8,12},{12,8},{16,20},{20,16},{24,28},{28,24},{1,5},{5... | collective-permute-start | bytes 1572872 | tf_op jit(solution)/shard_map/ppermute | solution.py:50
  171.5 16.2 %collective-permute-start.18 = (bf16[512,256]{1,0:T(8,128)(2,1)S(1)}, bf16[512,256]{1,0:T(8,128)(2,1)S(1)}, u32[]{:S(2)}, u32[]{:S(2)}) collective-permute-start(bf16[512,256]{1,0:T(8,128)(2,1)S(1)} %pad_maximum_fusion.20), channel_id=1, source_target_pairs={{0,4},{4,0},{8,12},{12,8},{16,20},{20,16},{24,28},{28,24},{1,5},{5... | collective-permute-start | bytes 786440 | tf_op jit(solution)/shard_map/ppermute | solution.py:50
  172.2 19.2 %collective-permute-start.26 = (bf16[2,256,256]{2,1,0:T(8,128)(2,1)S(1)}, bf16[2,256,256]{2,1,0:T(8,128)(2,1)S(1)}, u32[]{:S(2)}, u32[]{:S(2)}) collective-permute-start(bf16[2,256,256]{2,1,0:T(8,128)(2,1)S(1)} %get-tuple-element.29), channel_id=1, source_target_pairs={{0,8},{4,12},{8,0},{12,4},{16,24},{20,28},{24,16},{28,20},{1,9},{5... | collective-permute-start | bytes 786440 | tf_op jit(solution)/shard_map/ppermute | solution.py:50
  187.7 28.7 %collective-permute-start.30 = (bf16[512,1024]{1,0:T(8,128)(2,1)S(1)}, bf16[512,1024]{1,0:T(8,128)(2,1)S(1)}, u32[]{:S(2)}, u32[]{:S(2)}) collective-permute-start(bf16[512,1024]{1,0:T(8,128)(2,1)S(1)} %pad_maximum_fusion.12), channel_id=1, source_target_pairs={{0,4},{4,0},{8,12},{12,8},{16,20},{20,16},{24,28},{28,24},{1,5},{5... | collective-permute-start | bytes 3145736 | tf_op jit(solution)/shard_map/ppermute | solution.py:50
  190.1 6.4 %collective-permute-start.20 = (bf16[256,512]{1,0:T(8,128)(2,1)S(1)}, bf16[256,512]{1,0:T(8,128)(2,1)S(1)}, u32[]{:S(2)}, u32[]{:S(2)}) collective-permute-start(bf16[256,512]{1,0:T(8,128)(2,1)S(1)} %dynamic-slice_convert_fusion), channel_id=1, source_target_pairs={{0,8},{4,12},{8,0},{12,4},{16,24},{20,28},{24,16},{28,20},{1,9},{5... | collective-permute-start | bytes 786440 | tf_op jit(solution)/shard_map/ppermute | solution.py:50
  191.5 19.2 %collective-permute-start.27 = (bf16[2,512,128]{2,1,0:T(8,128)(2,1)S(1)}, bf16[2,512,128]{2,1,0:T(8,128)(2,1)S(1)}, u32[]{:S(2)}, u32[]{:S(2)}) collective-permute-start(bf16[2,512,128]{2,1,0:T(8,128)(2,1)S(1)} %get-tuple-element.27), channel_id=1, source_target_pairs={{0,4},{4,0},{8,12},{12,8},{16,20},{20,16},{24,28},{28,24},{1,5},{5... | collective-permute-start | bytes 786440 | tf_op jit(solution)/shard_map/ppermute | solution.py:50
  196.6 18.9 %collective-permute-start.21 = (bf16[128,512]{1,0:T(8,128)(2,1)S(1)}, bf16[128,512]{1,0:T(8,128)(2,1)S(1)}, u32[]{:S(2)}, u32[]{:S(2)}) collective-permute-start(bf16[128,512]{1,0:T(8,128)(2,1)S(1)} %dynamic-slice_convert_fusion.1), channel_id=1, source_target_pairs={{0,16},{4,20},{8,24},{12,28},{16,0},{20,4},{24,8},{28,12},{1,17},{... | collective-permute-start | bytes 393224 | tf_op jit(solution)/shard_map/ppermute | solution.py:50
  (60 other events, 326.3 us)

commit v3 on v2

--- a/solution.py
+++ b/solution.py
@@ -57,10 +57,9 @@
     return value
 
 
-def merge_totals(first, second):
-    top = jnp.maximum(first[0], second[0])
-    total = first[1] * jnp.exp(first[0] - top) + second[1] * jnp.exp(second[0] - top)
-    return top, total
+def merge_lse(first, second):
+    top = jnp.maximum(first, second)
+    return top + jnp.log(jnp.exp(first - top) + jnp.exp(second - top))
 
 
 def reverse_blocks(value):
@@ -91,21 +90,27 @@
     return total
 
 
-def gather_rows(value):
-    for step in reversed(range(axis_bits("dp"))):
-        value = jnp.concatenate([value, swap(value, "dp", step)], axis=0)
+def gather_rows(value, later=()):
+    for turn, step in enumerate(reversed(range(axis_bits("dp")))):
+        received = swap(value, "dp", step)
+        if turn < len(later):
+            value, received, _ = lax.optimization_barrier((value, received, later[turn]))
+        value = jnp.concatenate([value, received], axis=0)
     return value
 
 
-def gather_columns(value):
+def gather_columns(value, later=()):
     index = lax.axis_index("dp")
     width = value.shape[-1]
-    for step in reversed(range(axis_bits("dp"))):
+    for turn, step in enumerate(reversed(range(axis_bits("dp")))):
         width //= 2
         bit = (index >> step) & 1
         sent = lax.dynamic_slice_in_dim(value, (1 - bit) * width, width, value.ndim - 1)
         kept = lax.dynamic_slice_in_dim(value, bit * width, width, value.ndim - 1)
-        value = jnp.concatenate([kept, swap(sent, "dp", step)], axis=-2)
+        received = swap(sent, "dp", step)
+        if turn < len(later):
+            kept, received, _ = lax.optimization_barrier((kept, received, later[turn]))
+        value = jnp.concatenate([kept, received], axis=-2)
     return value
 
 
@@ -157,15 +162,6 @@
 
 def batch_tn(left, right):
     return jnp.einsum("bji,bjk->bik", left, right, preferred_element_type=jnp.float32)
-
-
-def masked_max(values, member):
-    return jnp.max(jnp.where(member, values[:, None], -1e30), axis=0)
-
-
-def masked_sum(values, member, top_value):
-    shifted = jnp.where(member, values[:, None] - top_value[None, :], -1e30)
-    return jnp.sum(jnp.where(member, jnp.exp(shifted), 0.0), axis=0)
 
 
 def per_pair(per_query, member):
@@ -210,8 +206,6 @@
     first_norm = layer_norm(pre_one).astype(jnp.bfloat16)
     inner_act = matmul(first_norm, up_weight)
     activated = gelu_tanh(inner_act).astype(jnp.bfloat16)
-    lefts = gather_rows(jnp.concatenate([activated, context], axis=1))
-    rights = gather_columns(jnp.stack([first_norm, picked_states]))
     pre_two = first_norm.astype(jnp.float32) + sum_over_mp(matmul(activated, down_weight))
     picked = layer_norm(pre_two).astype(jnp.bfloat16)
 
@@ -222,11 +216,17 @@
     top_value = jnp.max(logits, axis=1)
     denominator = jnp.sum(jnp.exp(logits - top_value[:, None]), axis=1)
     target_logit = jnp.sum(jnp.where(target_hot, logits, 0.0), axis=1)
+    stats = jnp.stack([top_value + jnp.log(denominator), target_logit])
+    is_lse = jnp.arange(2)[:, None] == 0
     for bit in range(axis_bits("mp")):
-        other = swap(jnp.stack([top_value, denominator, target_logit]), "mp", bit)
-        top_value, denominator = merge_totals((top_value, denominator), (other[0], other[1]))
-        target_logit = target_logit + other[2]
-    log_prob = target_logit - top_value - jnp.log(denominator)
+        other = swap(stats, "mp", bit)
+        stats = jnp.where(is_lse, merge_lse(stats, other), stats + other)
+    row_lse = stats[0]
+    log_prob = stats[1] - row_lse
+
+    later = (picked, row_lse)
+    lefts = gather_rows(jnp.concatenate([activated, context], axis=1), later)
+    rights = gather_columns(jnp.stack([first_norm, picked_states]), later)
     doc_ll = jnp.sum(log_prob.reshape(pairs_dev, mask_count), axis=1) / mask_count
 
     post_values = retrieval + doc_ll
@@ -235,28 +235,28 @@
         pair_query, lax.axis_index("dp") * pairs_dev, pairs_dev, 0
     )
     member = local_query[:, None] == jnp.arange(query_count)[None, :]
-    tops = jnp.stack([masked_max(post_values, member), masked_max(retrieval, member)])
-    totals = jnp.stack(
-        [masked_sum(post_values, member, tops[0]), masked_sum(retrieval, member, tops[1])]
-    )
+    scored = jnp.stack([post_values, retrieval])[:, :, None]
+    tops = jnp.max(jnp.where(member[None], scored, -1e30), axis=1)
+    shifted = jnp.where(member[None], scored - tops[:, None, :], -1e30)
+    totals = jnp.sum(jnp.where(member[None], jnp.exp(shifted), 0.0), axis=1)
+    present = jnp.any(member, axis=0)[None]
+    lse = jnp.where(present, tops + jnp.log(jnp.where(present, totals, 1.0)), -1e30)
     for bit in range(axis_bits("dp")):
-        other = swap(jnp.stack([tops, totals]), "dp", bit)
-        tops, totals = merge_totals((tops, totals), (other[0], other[1]))
-    lse = tops + jnp.log(totals)
+        lse = merge_lse(lse, swap(lse, "dp", bit))
     posterior = jnp.exp(post_values - per_pair(lse[0], member))
     prior = jnp.exp(retrieval - per_pair(lse[1], member))
     score_grad = prior - posterior
 
-    vocab_probs = jnp.exp(logits - top_value[:, None]) / denominator[:, None]
+    vocab_probs = jnp.exp(logits - row_lse[:, None])
     dlogit = (vocab_probs - target_hot.astype(jnp.float32)).astype(jnp.bfloat16)
     dpicked = sum_over_mp(matmul(dlogit, vocab_embed))
     dpicked = dpicked * (jnp.repeat(posterior, mask_count)[:, None] / mask_count)
 
     dpre_two = norm_back(pre_two, dpicked).astype(jnp.bfloat16)
     dinner = gelu_back(inner_act, matmul_nt(dpre_two, down_weight)).astype(jnp.bfloat16)
-    dinner_all = gather_rows(dinner)
     dfirst = dpre_two.astype(jnp.float32) + sum_over_mp(matmul_nt(dinner, up_weight))
     dpre_one = norm_back(pre_one, dfirst).astype(jnp.bfloat16)
+    dinner_all = gather_rows(dinner, (dpre_one,))
     dpre = gather_columns(jnp.stack([dpre_two, dpre_one]))
 
     dcontext = matmul_nt(dpre_one, out_weight).astype(jnp.bfloat16)
@@ -264,7 +264,7 @@
     dval = batch_tn(probs, dcontext).astype(jnp.bfloat16)
     dprobs = batch_nt(dcontext, val)
     dscores = soft * (dprobs - jnp.sum(soft * dprobs, axis=-1, keepdims=True))
-    dscores = (dscores * HEAD ** (-0.5)).astype(jnp.bfloat16)
+    dscores = lax.optimization_barrier((dscores * HEAD ** (-0.5)).astype(jnp.bfloat16))
     dkey = batch_tn(dscores, query).astype(jnp.bfloat16)
     dquery = join_heads(fold_heads(batch_nn(dscores, key)).astype(jnp.bfloat16), pairs_dev)
     dquery_all = gather_rows(dquery)

time: 220 us -> 196 us (0.89)
  matrix products: 47.2 us -> 29.4 us
  starting transfers between devices: 35.8 us -> 31 us
  local copies, waits for them, and re-layouts: 26.2 us -> 23.5 us
  waiting for transfers between devices: 86.5 us -> 89.1 us
    squeeze x6 -> x0, local copies, waits for them, and re-layouts: 7.78 us -> none  [the longest x2 2.67 us: local(): target_logit = target_logit + other[2]]
    dot_general x2, matrix products: 6.26 us -> 0.73 us  [batch_tn(): jnp.einsum('bji,bjk->bik', left, right, preferred_element_type=jnp.float32)]
    dot_general x2, matrix products: 7.42 us -> 2.08 us  [batch_nn(): jnp.einsum('bij,bjk->bik', left, right, preferred_element_type=jnp.float32)]
    ppermute x31, starting transfers between devices: 35.8 us -> 31 us  [swap(): return lax.ppermute(value, axis, pairs)]
    dot_general x7, matrix products: 11.7 us -> 7.64 us  [matmul(): return jnp.dot(left, right, preferred_element_type=jnp.float32)]
    unnamed x131 -> x128, local copies, waits for them, and re-layouts: 11 us -> 15 us
    concatenate x11 -> x8, other arithmetic: 6.34 us -> 2.62 us  [the longest x5 1.51 us: gather_rows(): value = jnp.concatenate([value, received], axis=0)]
    sub x0 -> x2, other arithmetic: none -> 3.34 us  [the longest x1 2.79 us: local(): dscores = soft * (dprobs - jnp.sum(soft * dprobs, axis=-1, keepdims=True))]
  transfers between devices with their start and end apart: 31 -> 31, of which waited for: 12 -> 18; matrix products, arithmetic and copies ran while one was open for 34% -> 29% of each run, Pallas kernels for 0% -> 0%
where the time goes in v3:
time: 196 us; the launch traced here: 195 us
  waiting for transfers between devices  89.1 us (45%)
  starting transfers between devices  31 us (16%)
  matrix products  29.4 us (15%)
  local copies, waits for them, and re-layouts  23.5 us (12%)
  other arithmetic  20.3 us (10%)
    ppermute x31, waiting for transfers between devices, swap(): return lax.ppermute(value, axis, pairs)  89.1 us
    ppermute x31, starting transfers between devices, swap(): return lax.ppermute(value, axis, pairs)  31 us
    unnamed x128, local copies, waits for them, and re-layouts  15 us
    dot_general x4, matrix products, matmul_nt(): lax.dot_general(left, right, (((1,), (1,)), ((), ())), preferred_element_...  8.67 us
    dot_general x6, matrix products, matmul_tn(): lax.dot_general(left, right, (((0,), (0,)), ((), ())), preferred_element_...  8.07 us
    dot_general x7, matrix products, matmul(): return jnp.dot(left, right, preferred_element_type=jnp.float32)  7.64 us
  transfers between devices with their start and end apart: 31, of which 18 were waited for; matrix products, arithmetic and copies ran while one was open for 29% of the time, Pallas kernels for 0%

profile of v3, /device:TPU:0, one launch (start us, length us, event | category | flops | bytes accessed | tf_op | source)
XLA Modules:
  0.0 194.9 jit_solution(16878001448047455914)
XLA Ops:
  0.7 2.5 %convolution_convert_fusion.2 = bf16[1024,256]{1,0:T(8,128)(2,1)S(1)} fusion(bf16[1024,1024]{1,0:T(8,128)(2,1)} %bitcast.149, bf16[3,1024,256]{2,1,0:T(8,128)(2,1)} %param.15), kind=kOutput, calls=%fused_computation.25 | convolution fusion | flops 537133056 | bytes 3145728 | tf_op jit(solution)/shard_map/dot_general | solution.py:10
  8.2 1.8 fusion.62
  15.6 1.7 slice_dynamic-update-slice_fusion.2
  17.4 2.6 %collective-permute-start.1 = (bf16[128,1024]{1,0:T(8,128)(2,1)S(1)}, bf16[128,1024]{1,0:T(8,128)(2,1)S(1)}, u32[]{:S(2)}, u32[]{:S(2)}) collective-permute-start(bf16[128,1024]{1,0:T(8,128)(2,1)S(1)} %add_convert_fusion.5), channel_id=1, source_target_pairs={{0,2},{1,3},{2,0},{3,1},{4,6},{5,7},{6,4},{7,5},{8,10},{9,11},{10,... | collective-permute-start | bytes 786440 | tf_op jit(solution)/shard_map/ppermute | solution.py:50
  21.1 1.7 slice_dynamic-update-slice_fusion.1
  22.8 4.1 %collective-permute-done.1 = bf16[128,1024]{1,0:T(8,128)(2,1)S(1)} collective-permute-done((bf16[128,1024]{1,0:T(8,128)(2,1)S(1)}, bf16[128,1024]{1,0:T(8,128)(2,1)S(1)}, u32[]{:S(2)}, u32[]{:S(2)}) %collective-permute-start.1) | collective-permute-done | bytes 262176 | tf_op jit(solution)/shard_map/ppermute | solution.py:50
  32.4 1.8 slice_dynamic-update-slice_fusion
  35.2 1.8 collective-permute-start.4
  37.0 2.7 %collective-permute-start.2 = (bf16[2,128,512]{2,1,0:T(8,128)(2,1)S(1)}, bf16[2,128,512]{2,1,0:T(8,128)(2,1)S(1)}, u32[]{:S(2)}, u32[]{:S(2)}) collective-permute-start(bf16[2,128,512]{2,1,0:T(8,128)(2,1)S(1)} %get-tuple-element.43), channel_id=1, source_target_pairs={{0,16},{4,20},{8,24},{12,28},{16,0},{20,4},{24,8},{28,12},{1,17},{... | collective-permute-start | bytes 786440 | tf_op jit(solution)/shard_map/ppermute | solution.py:50
  41.1 2.9 %collective-permute-done.4 = bf16[128,1024]{1,0:T(8,128)(2,1)S(1)} collective-permute-done((bf16[128,1024]{1,0:T(8,128)(2,1)S(1)}, bf16[128,1024]{1,0:T(8,128)(2,1)S(1)}, u32[]{:S(2)}, u32[]{:S(2)}) %collective-permute-start.4) | collective-permute-done | bytes 262176 | tf_op jit(solution)/shard_map/ppermute | solution.py:50
  45.1 6.5 %fusion.107 = (f32[128]{0:T(128)S(1)}, f32[128,4096]{1,0:T(8,128)S(1)}) fusion(bf16[128,1024]{1,0:T(8,128)(2,1)S(1)} %multiply_convert_fusion, bf16[4096,1024]{1,0:T(8,128)(2,1)} %param.19), kind=kOutput, calls=%fused_computation.293 | convolution fusion | flops 1074265984 | bytes 10748416 | tf_op jit(solution)/shard_map/dot_general | solution.py:20
  52.4 7.3 %collective-permute-done.2 = bf16[2,128,512]{2,1,0:T(8,128)(2,1)S(1)} collective-permute-done((bf16[2,128,512]{2,1,0:T(8,128)(2,1)S(1)}, bf16[2,128,512]{2,1,0:T(8,128)(2,1)S(1)}, u32[]{:S(2)}, u32[]{:S(2)}) %collective-permute-start.2) | collective-permute-done | bytes 262176 | tf_op jit(solution)/shard_map/ppermute | solution.py:50
  60.7 5.5 %collective-permute-done.22 = bf16[128,1280]{1,0:T(8,128)(2,1)S(1)} collective-permute-done((bf16[128,1280]{1,0:T(8,128)(2,1)S(1)}, bf16[128,1280]{1,0:T(8,128)(2,1)S(1)}, u32[]{:S(2)}, u32[]{:S(2)}) %collective-permute-start.22) | collective-permute-done | bytes 327712 | tf_op jit(solution)/shard_map/ppermute | solution.py:50
  68.9 1.7 collective-permute-done.7
  71.2 2.2 %convolution_convert_fusion.6 = bf16[128,1024]{1,0:T(8,128)(2,1)} fusion(bf16[4096,1024]{1,0:T(8,128)(2,1)S(1)} %bitcast.145, f32[128,4096]{1,0:T(8,128)S(1)} %get-tuple-element.96, f32[128]{0:T(128)S(1)} %get-tuple-element.88, s32[128]{0:T(128)S(1)} %copy-done.38), kind=kOutput, calls=%fused_computation.30 | convolution fusion | flops 1076494336 | bytes 10748928 | tf_op jit(solution)/shard_map/dot_general | solution.py:10
  79.0 2.1 %collective-permute-done.11 = f32[2,2]{1,0:T(2,128)S(1)} collective-permute-done((f32[2,2]{1,0:T(2,128)S(1)}, f32[2,2]{1,0:T(2,128)S(1)}, u32[]{:S(2)}, u32[]{:S(2)}) %collective-permute-start.11) | collective-permute-done | bytes 48 | tf_op jit(solution)/shard_map/ppermute | solution.py:50
  81.8 4.0 %collective-permute-done.12 = f32[2,2]{1,0:T(2,128)S(1)} collective-permute-done((f32[2,2]{1,0:T(2,128)S(1)}, f32[2,2]{1,0:T(2,128)S(1)}, u32[]{:S(2)}, u32[]{:S(2)}) %collective-permute-start.12) | collective-permute-done | bytes 48 | tf_op jit(solution)/shard_map/ppermute | solution.py:50
  87.5 2.9 %collective-permute-done.13 = f32[2,2]{1,0:T(2,128)S(1)} collective-permute-done((f32[2,2]{1,0:T(2,128)S(1)}, f32[2,2]{1,0:T(2,128)S(1)}, u32[]{:S(2)}, u32[]{:S(2)}) %collective-permute-start.13) | collective-permute-done | bytes 48 | tf_op jit(solution)/shard_map/ppermute | solution.py:50
  97.9 2.6 %collective-permute-done.10 = bf16[128,1024]{1,0:T(8,128)(2,1)S(1)} collective-permute-done((bf16[128,1024]{1,0:T(8,128)(2,1)S(1)}, bf16[128,1024]{1,0:T(8,128)(2,1)S(1)}, u32[]{:S(2)}, u32[]{:S(2)}) %collective-permute-start.10) | collective-permute-done | bytes 262176 | tf_op jit(solution)/shard_map/ppermute | solution.py:50
  111.5 3.9 %collective-permute-done.15 = bf16[128,1024]{1,0:T(8,128)(2,1)S(1)} collective-permute-done((bf16[128,1024]{1,0:T(8,128)(2,1)S(1)}, bf16[128,1024]{1,0:T(8,128)(2,1)S(1)}, u32[]{:S(2)}, u32[]{:S(2)}) %collective-permute-start.15) | collective-permute-done | bytes 262176 | tf_op jit(solution)/shard_map/ppermute | solution.py:50
  118.1 2.8 %fusion.17 = bf16[4,128,512]{2,1,0:T(8,128)(2,1)S(1)} fusion(f32[4,128,512]{2,1,0:T(8,128)S(1)} %fusion.67, f32[4,128,512]{2,1,0:T(8,128)S(1)} %copy-done.52, f32[4,128]{1,0:T(4,128)S(1)} %copy-done.54), kind=kOutput, calls=%fused_computation.27 | output fusion | flops 1836031 | bytes 2623488 | tf_op jit(solution)/shard_map/sub | solution.py:266
  121.8 2.0 %convolution_convert_fusion.4 = bf16[512,512]{1,0:T(8,128)(2,1)S(1)} fusion(bf16[1024,1024]{1,0:T(8,128)(2,1)} %slice_dynamic-update-slice_fusion, s32[]{:T(128)S(6)} %select_n.147, bf16[512,128]{0,1:T(8,128)(2,1)S(1)} %get-tuple-element.50, bf16[512,128]{0,1:T(8,128)(2,1)S(1)} %get-tuple-element.51, bf16[512,128]{0,1:T(8,128)(2,1)S(1)} %get-tuple-element.52, ...), kind=kOutput, calls=%fused_computation.28 | convolution fusion | flops 545521664 | bytes 2621444 | tf_op jit(solution)/shard_map/dot_general | solution.py:14
  126.9 4.4 %collective-permute-done.16 = bf16[128,256]{1,0:T(8,128)(2,1)S(1)} collective-permute-done((bf16[128,256]{1,0:T(8,128)(2,1)S(1)}, bf16[128,256]{1,0:T(8,128)(2,1)S(1)}, u32[]{:S(2)}, u32[]{:S(2)}) %collective-permute-start.16) | collective-permute-done | bytes 65568 | tf_op jit(solution)/shard_map/ppermute | solution.py:50
  131.4 1.9 collective-permute-start.17
  134.3 3.3 %collective-permute-done.17 = bf16[256,256]{1,0:T(8,128)(2,1)S(1)} collective-permute-done((bf16[256,256]{1,0:T(8,128)(2,1)S(1)}, bf16[256,256]{1,0:T(8,128)(2,1)S(1)}, u32[]{:S(2)}, u32[]{:S(2)}) %collective-permute-start.17) | collective-permute-done | bytes 131104 | tf_op jit(solution)/shard_map/ppermute | solution.py:50
  138.2 7.6 %collective-permute-done.25 = bf16[2,128,512]{2,1,0:T(8,128)(2,1)S(1)} collective-permute-done((bf16[2,128,512]{2,1,0:T(8,128)(2,1)S(1)}, bf16[2,128,512]{2,1,0:T(8,128)(2,1)S(1)}, u32[]{:S(2)}, u32[]{:S(2)}) %collective-permute-start.25) | collective-permute-done | bytes 262176 | tf_op jit(solution)/shard_map/ppermute | solution.py:50
  145.9 10.7 %collective-permute-done.18 = bf16[512,256]{1,0:T(8,128)(2,1)S(1)} collective-permute-done((bf16[512,256]{1,0:T(8,128)(2,1)S(1)}, bf16[512,256]{1,0:T(8,128)(2,1)S(1)}, u32[]{:S(2)}, u32[]{:S(2)}) %collective-permute-start.18) | collective-permute-done | bytes 262176 | tf_op jit(solution)/shard_map/ppermute | solution.py:50
  156.6 1.8 collective-permute-start.26
  158.8 2.0 %convert_add_fusion = f32[512,512]{1,0:T(8,128)S(1)} fusion(bf16[512,512]{1,0:T(8,128)(2,1)S(1)} %collective-permute-done.19, bf16[1024,1024]{1,0:T(8,128)(2,1)} %slice_dynamic-update-slice_fusion, s32[]{:T(128)S(6)} %select_n.146, bf16[512,128]{0,1:T(8,128)(2,1)S(1)} %get-tuple-element.50, bf16[512,128]{0,1:T(8,128)(2,1)S(1)} %get-tuple-element.51, ...), kind=kOutput, calls=%fused_computation.39 | convolution fusion | flops 545783808 | bytes 3670020 | tf_op jit(solution)/shard_map/dot_general | solution.py:14
  161.1 4.8 %collective-permute-done.26 = bf16[2,256,256]{2,1,0:T(8,128)(2,1)S(1)} collective-permute-done((bf16[2,256,256]{2,1,0:T(8,128)(2,1)S(1)}, bf16[2,256,256]{2,1,0:T(8,128)(2,1)S(1)}, u32[]{:S(2)}, u32[]{:S(2)}) %collective-permute-start.26) | collective-permute-done | bytes 262176 | tf_op jit(solution)/shard_map/ppermute | solution.py:50
  170.8 4.4 %collective-permute-done.27 = bf16[2,512,128]{2,1,0:T(8,128)(2,1)S(1)} collective-permute-done((bf16[2,512,128]{2,1,0:T(8,128)(2,1)S(1)}, bf16[2,512,128]{2,1,0:T(8,128)(2,1)S(1)}, u32[]{:S(2)}, u32[]{:S(2)}) %collective-permute-start.27) | collective-permute-done | bytes 262176 | tf_op jit(solution)/shard_map/ppermute | solution.py:50
  178.7 15.0 %collective-permute-done.30 = bf16[512,1024]{1,0:T(8,128)(2,1)S(1)} collective-permute-done((bf16[512,1024]{1,0:T(8,128)(2,1)S(1)}, bf16[512,1024]{1,0:T(8,128)(2,1)S(1)}, u32[]{:S(2)}, u32[]{:S(2)}) %collective-permute-start.30) | collective-permute-done | bytes 1048608 | tf_op jit(solution)/shard_map/ppermute | solution.py:50
  (275 shorter events, 70.2 us)
Async XLA Ops:
  0.6 28.0 %copy-start = (bf16[1024,1024]{1,0:T(8,128)(2,1)S(1)}, bf16[1024,1024]{1,0:T(8,128)(2,1)}, u32[]{:S(2)}) copy-start(bf16[1024,1024]{1,0:T(8,128)(2,1)} %param.17) | copy-start | bytes 6291460
  10.3 6.9 %collective-permute-start = (bf16[128,1024]{1,0:T(8,128)(2,1)S(1)}, bf16[128,1024]{1,0:T(8,128)(2,1)S(1)}, u32[]{:S(2)}, u32[]{:S(2)}) collective-permute-start(bf16[128,1024]{1,0:T(8,128)(2,1)S(1)} %convolution_convert_fusion.8), channel_id=1, source_target_pairs={{0,1},{1,0},{2,3},{3,2},{4,5},{5,4},{6,7},{7,6},{8,9},{9,8},{10,11... | collective-permute-start | bytes 786440 | tf_op jit(solution)/shard_map/ppermute | solution.py:50
  17.4 9.6 %collective-permute-start.1 = (bf16[128,1024]{1,0:T(8,128)(2,1)S(1)}, bf16[128,1024]{1,0:T(8,128)(2,1)S(1)}, u32[]{:S(2)}, u32[]{:S(2)}) collective-permute-start(bf16[128,1024]{1,0:T(8,128)(2,1)S(1)} %add_convert_fusion.5), channel_id=1, source_target_pairs={{0,2},{1,3},{2,0},{3,1},{4,6},{5,7},{6,4},{7,5},{8,10},{9,11},{10,... | collective-permute-start | bytes 786440 | tf_op jit(solution)/shard_map/ppermute | solution.py:50
  30.5 3.7 %collective-permute-start.3 = (bf16[128,1024]{1,0:T(8,128)(2,1)S(1)}, bf16[128,1024]{1,0:T(8,128)(2,1)}, u32[]{:S(2)}, u32[]{:S(2)}) collective-permute-start(bf16[128,1024]{1,0:T(8,128)(2,1)S(1)} %convolution_convert_fusion.7), channel_id=1, source_target_pairs={{0,1},{1,0},{2,3},{3,2},{4,5},{5,4},{6,7},{7,6},{8,9},{9,8},{10,11... | collective-permute-start | bytes 786440 | tf_op jit(solution)/shard_map/ppermute | solution.py:50
  35.2 8.8 %collective-permute-start.4 = (bf16[128,1024]{1,0:T(8,128)(2,1)S(1)}, bf16[128,1024]{1,0:T(8,128)(2,1)S(1)}, u32[]{:S(2)}, u32[]{:S(2)}) collective-permute-start(bf16[128,1024]{1,0:T(8,128)(2,1)S(1)} %add_convert_fusion.4), channel_id=1, source_target_pairs={{0,2},{1,3},{2,0},{3,1},{4,6},{5,7},{6,4},{7,5},{8,10},{9,11},{10,... | collective-permute-start | bytes 786440 | tf_op jit(solution)/shard_map/ppermute | solution.py:50
  37.0 22.7 %collective-permute-start.2 = (bf16[2,128,512]{2,1,0:T(8,128)(2,1)S(1)}, bf16[2,128,512]{2,1,0:T(8,128)(2,1)S(1)}, u32[]{:S(2)}, u32[]{:S(2)}) collective-permute-start(bf16[2,128,512]{2,1,0:T(8,128)(2,1)S(1)} %get-tuple-element.43), channel_id=1, source_target_pairs={{0,16},{4,20},{8,24},{12,28},{16,0},{20,4},{24,8},{28,12},{1,17},{... | collective-permute-start | bytes 786440 | tf_op jit(solution)/shard_map/ppermute | solution.py:50
  40.7 25.5 %collective-permute-start.22 = (bf16[128,1280]{1,0:T(8,128)(2,1)S(1)}, bf16[128,1280]{1,0:T(8,128)(2,1)S(1)}, u32[]{:S(2)}, u32[]{:S(2)}) collective-permute-start(bf16[128,1280]{1,0:T(8,128)(2,1)S(1)} %maximum_maximum_fusion.1), channel_id=1, source_target_pairs={{0,16},{4,20},{8,24},{12,28},{16,0},{20,4},{24,8},{28,12},{1,17},{... | collective-permute-start | bytes 983048 | tf_op jit(solution)/shard_map/ppermute | solution.py:50
  52.3 14.6 %collective-permute-start.6 = (f32[2,128]{1,0:T(2,128)S(1)}, f32[2,128]{1,0:T(2,128)S(1)}, u32[]{:S(2)}, u32[]{:S(2)}) collective-permute-start(f32[2,128]{1,0:T(2,128)S(1)} %pad_maximum_fusion.30), channel_id=1, source_target_pairs={{0,1},{1,0},{2,3},{3,2},{4,5},{5,4},{6,7},{7,6},{8,9},{9,8},{10,11... | collective-permute-start | bytes 3080 | tf_op jit(solution)/shard_map/ppermute | solution.py:50
  60.7 32.0 %collective-permute-start.5 = (bf16[2,256,256]{2,1,0:T(8,128)(2,1)}, bf16[2,256,256]{2,1,0:T(8,128)(2,1)}, u32[]{:S(2)}, u32[]{:S(2)}) collective-permute-start(bf16[2,256,256]{2,1,0:T(8,128)(2,1)} %get-tuple-element.41), channel_id=1, source_target_pairs={{0,8},{4,12},{8,0},{12,4},{16,24},{20,28},{24,16},{28,20},{1,9},{5... | collective-permute-start | bytes 786440 | tf_op jit(solution)/shard_map/ppermute | solution.py:50
  67.0 3.6 %collective-permute-start.7 = (f32[2,128]{1,0:T(2,128)S(1)}, f32[2,128]{1,0:T(2,128)S(1)}, u32[]{:S(2)}, u32[]{:S(2)}) collective-permute-start(f32[2,128]{1,0:T(2,128)S(1)} %add_select_fusion.2), channel_id=1, source_target_pairs={{0,2},{1,3},{2,0},{3,1},{4,6},{5,7},{6,4},{7,5},{8,10},{9,11},{10,... | collective-permute-start | bytes 3080 | tf_op jit(solution)/shard_map/ppermute | solution.py:50
  68.2 36.9 %collective-permute-start.23 = (bf16[256,1280]{1,0:T(8,128)(2,1)}, bf16[256,1280]{1,0:T(8,128)(2,1)}, u32[]{:S(2)}, u32[]{:S(2)}) collective-permute-start(bf16[256,1280]{1,0:T(8,128)(2,1)} %constant_dynamic-update-slice_fusion.9), channel_id=1, source_target_pairs={{0,8},{4,12},{8,0},{12,4},{16,24},{20,28},{24,16},{28,20},{1,9},{5... | collective-permute-start | bytes 1966088 | tf_op jit(solution)/shard_map/ppermute | solution.py:50
  73.5 19.2 %collective-permute-start.9 = (bf16[128,1024]{1,0:T(8,128)(2,1)}, bf16[128,1024]{1,0:T(8,128)(2,1)}, u32[]{:S(2)}, u32[]{:S(2)}) collective-permute-start(bf16[128,1024]{1,0:T(8,128)(2,1)} %convolution_convert_fusion.6), channel_id=1, source_target_pairs={{0,1},{1,0},{2,3},{3,2},{4,5},{5,4},{6,7},{7,6},{8,9},{9,8},{10,11... | collective-permute-start | bytes 786440 | tf_op jit(solution)/shard_map/ppermute | solution.py:50
  77.5 3.6 %collective-permute-start.11 = (f32[2,2]{1,0:T(2,128)S(1)}, f32[2,2]{1,0:T(2,128)S(1)}, u32[]{:S(2)}, u32[]{:S(2)}) collective-permute-start(f32[2,2]{1,0:T(2,128)S(1)} %add_select_fusion), channel_id=1, source_target_pairs={{0,4},{4,0},{8,12},{12,8},{16,20},{20,16},{24,28},{28,24},{1,5},{5... | collective-permute-start | bytes 56 | tf_op jit(solution)/shard_map/ppermute | solution.py:50
  81.1 4.7 %collective-permute-start.12 = (f32[2,2]{1,0:T(2,128)S(1)}, f32[2,2]{1,0:T(2,128)S(1)}, u32[]{:S(2)}, u32[]{:S(2)}) collective-permute-start(f32[2,2]{1,0:T(2,128)S(1)} %log_add_fusion.2), channel_id=1, source_target_pairs={{0,8},{4,12},{8,0},{12,4},{16,24},{20,28},{24,16},{28,20},{1,9},{5... | collective-permute-start | bytes 56 | tf_op jit(solution)/shard_map/ppermute | solution.py:50
  85.9 4.5 %collective-permute-start.13 = (f32[2,2]{1,0:T(2,128)S(1)}, f32[2,2]{1,0:T(2,128)S(1)}, u32[]{:S(2)}, u32[]{:S(2)}) collective-permute-start(f32[2,2]{1,0:T(2,128)S(1)} %log_add_fusion.1), channel_id=1, source_target_pairs={{0,16},{4,20},{8,24},{12,28},{16,0},{20,4},{24,8},{28,12},{1,17},{... | collective-permute-start | bytes 56 | tf_op jit(solution)/shard_map/ppermute | solution.py:50
  93.7 6.9 %collective-permute-start.10 = (bf16[128,1024]{1,0:T(8,128)(2,1)S(1)}, bf16[128,1024]{1,0:T(8,128)(2,1)S(1)}, u32[]{:S(2)}, u32[]{:S(2)}) collective-permute-start(bf16[128,1024]{1,0:T(8,128)(2,1)S(1)} %add_convert_fusion.3), channel_id=1, source_target_pairs={{0,2},{1,3},{2,0},{3,1},{4,6},{5,7},{6,4},{7,5},{8,10},{9,11},{10,... | collective-permute-start | bytes 786440 | tf_op jit(solution)/shard_map/ppermute | solution.py:50
  96.3 62.1 %collective-permute-start.8 = (bf16[2,512,128]{2,1,0:T(8,128)(2,1)S(1)}, bf16[2,512,128]{2,1,0:T(8,128)(2,1)S(1)}, u32[]{:S(2)}, u32[]{:S(2)}) collective-permute-start(bf16[2,512,128]{2,1,0:T(8,128)(2,1)S(1)} %get-tuple-element.39), channel_id=1, source_target_pairs={{0,4},{4,0},{8,12},{12,8},{16,20},{20,16},{24,28},{28,24},{1,5},{5... | collective-permute-start | bytes 786440 | tf_op jit(solution)/shard_map/ppermute | solution.py:50
  102.5 30.7 %collective-permute-start.28 = (bf16[128,1024]{1,0:T(8,128)(2,1)S(1)}, bf16[128,1024]{1,0:T(8,128)(2,1)S(1)}, u32[]{:S(2)}, u32[]{:S(2)}) collective-permute-start(bf16[128,1024]{1,0:T(8,128)(2,1)S(1)} %fusion.32), channel_id=1, source_target_pairs={{0,16},{4,20},{8,24},{12,28},{16,0},{20,4},{24,8},{28,12},{1,17},{... | collective-permute-start | bytes 786440 | tf_op jit(solution)/shard_map/ppermute | solution.py:50
  104.9 1.6 collective-permute-start.14
  106.6 8.8 %collective-permute-start.15 = (bf16[128,1024]{1,0:T(8,128)(2,1)S(1)}, bf16[128,1024]{1,0:T(8,128)(2,1)S(1)}, u32[]{:S(2)}, u32[]{:S(2)}) collective-permute-start(bf16[128,1024]{1,0:T(8,128)(2,1)S(1)} %add_convert_fusion.1), channel_id=1, source_target_pairs={{0,2},{1,3},{2,0},{3,1},{4,6},{5,7},{6,4},{7,5},{8,10},{9,11},{10,... | collective-permute-start | bytes 786440 | tf_op jit(solution)/shard_map/ppermute | solution.py:50
  108.8 61.9 %collective-permute-start.24 = (bf16[512,1280]{1,0:T(8,128)(2,1)S(1)}, bf16[512,1280]{1,0:T(8,128)(2,1)S(1)}, u32[]{:S(2)}, u32[]{:S(2)}) collective-permute-start(bf16[512,1280]{1,0:T(8,128)(2,1)S(1)} %pad_maximum_fusion), channel_id=1, source_target_pairs={{0,4},{4,0},{8,12},{12,8},{16,20},{20,16},{24,28},{28,24},{1,5},{5... | collective-permute-start | bytes 3932168 | tf_op jit(solution)/shard_map/ppermute | solution.py:50
  123.8 35.0 %collective-permute-start.19 = (bf16[512,512]{1,0:T(8,128)(2,1)S(1)}, bf16[512,512]{1,0:T(8,128)(2,1)S(1)}, u32[]{:S(2)}, u32[]{:S(2)}) collective-permute-start(bf16[512,512]{1,0:T(8,128)(2,1)S(1)} %convolution_convert_fusion.4), channel_id=1, source_target_pairs={{0,4},{4,0},{8,12},{12,8},{16,20},{20,16},{24,28},{28,24},{1,5},{5... | collective-permute-start | bytes 1572872 | tf_op jit(solution)/shard_map/ppermute | solution.py:50
  125.4 5.9 %collective-permute-start.16 = (bf16[128,256]{1,0:T(8,128)(2,1)S(1)}, bf16[128,256]{1,0:T(8,128)(2,1)S(1)}, u32[]{:S(2)}, u32[]{:S(2)}) collective-permute-start(bf16[128,256]{1,0:T(8,128)(2,1)S(1)} %maximum_maximum_fusion.2), channel_id=1, source_target_pairs={{0,16},{4,20},{8,24},{12,28},{16,0},{20,4},{24,8},{28,12},{1,17},{... | collective-permute-start | bytes 196616 | tf_op jit(solution)/shard_map/ppermute | solution.py:50
  131.4 6.3 %collective-permute-start.17 = (bf16[256,256]{1,0:T(8,128)(2,1)S(1)}, bf16[256,256]{1,0:T(8,128)(2,1)S(1)}, u32[]{:S(2)}, u32[]{:S(2)}) collective-permute-start(bf16[256,256]{1,0:T(8,128)(2,1)S(1)} %pad_maximum_fusion.11), channel_id=1, source_target_pairs={{0,8},{4,12},{8,0},{12,4},{16,24},{20,28},{24,16},{28,20},{1,9},{5... | collective-permute-start | bytes 393224 | tf_op jit(solution)/shard_map/ppermute | solution.py:50
  133.2 12.6 %collective-permute-start.25 = (bf16[2,128,512]{2,1,0:T(8,128)(2,1)S(1)}, bf16[2,128,512]{2,1,0:T(8,128)(2,1)S(1)}, u32[]{:S(2)}, u32[]{:S(2)}) collective-permute-start(bf16[2,128,512]{2,1,0:T(8,128)(2,1)S(1)} %get-tuple-element.37), channel_id=1, source_target_pairs={{0,16},{4,20},{8,24},{12,28},{16,0},{20,4},{24,8},{28,12},{1,17},{... | collective-permute-start | bytes 786440 | tf_op jit(solution)/shard_map/ppermute | solution.py:50
  137.6 19.0 %collective-permute-start.18 = (bf16[512,256]{1,0:T(8,128)(2,1)S(1)}, bf16[512,256]{1,0:T(8,128)(2,1)S(1)}, u32[]{:S(2)}, u32[]{:S(2)}) collective-permute-start(bf16[512,256]{1,0:T(8,128)(2,1)S(1)} %pad_maximum_fusion.8), channel_id=1, source_target_pairs={{0,4},{4,0},{8,12},{12,8},{16,20},{20,16},{24,28},{28,24},{1,5},{5... | collective-permute-start | bytes 786440 | tf_op jit(solution)/shard_map/ppermute | solution.py:50
  145.9 21.7 %collective-permute-start.29 = (bf16[256,1024]{1,0:T(8,128)(2,1)S(1)}, bf16[256,1024]{1,0:T(8,128)(2,1)S(1)}, u32[]{:S(2)}, u32[]{:S(2)}) collective-permute-start(bf16[256,1024]{1,0:T(8,128)(2,1)S(1)} %pad_maximum_fusion.4), channel_id=1, source_target_pairs={{0,8},{4,12},{8,0},{12,4},{16,24},{20,28},{24,16},{28,20},{1,9},{5... | collective-permute-start | bytes 1572872 | tf_op jit(solution)/shard_map/ppermute | solution.py:50
  156.6 9.2 %collective-permute-start.26 = (bf16[2,256,256]{2,1,0:T(8,128)(2,1)S(1)}, bf16[2,256,256]{2,1,0:T(8,128)(2,1)S(1)}, u32[]{:S(2)}, u32[]{:S(2)}) collective-permute-start(bf16[2,256,256]{2,1,0:T(8,128)(2,1)S(1)} %get-tuple-element.35), channel_id=1, source_target_pairs={{0,8},{4,12},{8,0},{12,4},{16,24},{20,28},{24,16},{28,20},{1,9},{5... | collective-permute-start | bytes 786440 | tf_op jit(solution)/shard_map/ppermute | solution.py:50
  160.8 9.1 %collective-permute-start.20 = (bf16[256,512]{1,0:T(8,128)(2,1)S(1)}, bf16[256,512]{1,0:T(8,128)(2,1)S(1)}, u32[]{:S(2)}, u32[]{:S(2)}) collective-permute-start(bf16[256,512]{1,0:T(8,128)(2,1)S(1)} %dynamic-slice_convert_fusion), channel_id=1, source_target_pairs={{0,8},{4,12},{8,0},{12,4},{16,24},{20,28},{24,16},{28,20},{1,9},{5... | collective-permute-start | bytes 786440 | tf_op jit(solution)/shard_map/ppermute | solution.py:50
  166.0 9.3 %collective-permute-start.27 = (bf16[2,512,128]{2,1,0:T(8,128)(2,1)S(1)}, bf16[2,512,128]{2,1,0:T(8,128)(2,1)S(1)}, u32[]{:S(2)}, u32[]{:S(2)}) collective-permute-start(bf16[2,512,128]{2,1,0:T(8,128)(2,1)S(1)} %get-tuple-element.33), channel_id=1, source_target_pairs={{0,4},{4,0},{8,12},{12,8},{16,20},{20,16},{24,28},{28,24},{1,5},{5... | collective-permute-start | bytes 786440 | tf_op jit(solution)/shard_map/ppermute | solution.py:50
  167.6 26.0 %collective-permute-start.30 = (bf16[512,1024]{1,0:T(8,128)(2,1)S(1)}, bf16[512,1024]{1,0:T(8,128)(2,1)S(1)}, u32[]{:S(2)}, u32[]{:S(2)}) collective-permute-start(bf16[512,1024]{1,0:T(8,128)(2,1)S(1)} %pad_maximum_fusion.1), channel_id=1, source_target_pairs={{0,4},{4,0},{8,12},{12,8},{16,20},{20,16},{24,28},{28,24},{1,5},{5... | collective-permute-start | bytes 3145736 | tf_op jit(solution)/shard_map/ppermute | solution.py:50
  170.0 7.8 %collective-permute-start.21 = (bf16[128,512]{1,0:T(8,128)(2,1)S(1)}, bf16[128,512]{1,0:T(8,128)(2,1)S(1)}, u32[]{:S(2)}, u32[]{:S(2)}) collective-permute-start(bf16[128,512]{1,0:T(8,128)(2,1)S(1)} %dynamic-slice_convert_fusion.1), channel_id=1, source_target_pairs={{0,16},{4,20},{8,24},{12,28},{16,0},{20,4},{24,8},{28,12},{1,17},{... | collective-permute-start | bytes 393224 | tf_op jit(solution)/shard_map/ppermute | solution.py:50
  (56 other events, 281.6 us)

commit v4 on v3

--- a/solution.py
+++ b/solution.py
@@ -90,8 +90,9 @@
     return total
 
 
-def gather_rows(value, later=()):
-    for turn, step in enumerate(reversed(range(axis_bits("dp")))):
+def gather_rows(value, later=(), first=None, last=0):
+    first = axis_bits("dp") if first is None else first
+    for turn, step in enumerate(reversed(range(last, first))):
         received = swap(value, "dp", step)
         if turn < len(later):
             value, received, _ = lax.optimization_barrier((value, received, later[turn]))
@@ -256,7 +257,7 @@
     dinner = gelu_back(inner_act, matmul_nt(dpre_two, down_weight)).astype(jnp.bfloat16)
     dfirst = dpre_two.astype(jnp.float32) + sum_over_mp(matmul_nt(dinner, up_weight))
     dpre_one = norm_back(pre_one, dfirst).astype(jnp.bfloat16)
-    dinner_all = gather_rows(dinner, (dpre_one,))
+    dinner_part = gather_rows(dinner, (dpre_one,), last=1)
     dpre = gather_columns(jnp.stack([dpre_two, dpre_one]))
 
     dcontext = matmul_nt(dpre_one, out_weight).astype(jnp.bfloat16)
@@ -269,6 +270,8 @@
     dquery = join_heads(fold_heads(batch_nn(dscores, key)).astype(jnp.bfloat16), pairs_dev)
     dquery_all = gather_rows(dquery)
     dkey_val = jnp.concatenate([join_heads(dkey, pairs_dev), join_heads(dval, pairs_dev)], axis=1)
+    dkey_val, dinner_part, lefts = lax.optimization_barrier((dkey_val, dinner_part, lefts))
+    dinner_all = gather_rows(dinner_part, first=1)
     key_val_grad = scatter_sum(reverse_blocks(flat_rows), dkey_val)
 
     ff_width = activated.shape[1]

time: 196 us -> 200 us (1.020)
  waiting for transfers between devices: 89.1 us -> 78 us
  starting transfers between devices: 31 us -> 38.7 us
  other arithmetic: 20.3 us -> 24.3 us
  local copies, waits for them, and re-layouts: 23.5 us -> 26.4 us
    ppermute x31, waiting for transfers between devices: 89.1 us -> 78 us  [swap(): return lax.ppermute(value, axis, pairs)]
    ppermute x31, starting transfers between devices: 31 us -> 38.7 us  [swap(): return lax.ppermute(value, axis, pairs)]
    dot_general x7, matrix products: 7.64 us -> 10.9 us  [matmul(): return jnp.dot(left, right, preferred_element_type=jnp.float32)]
    unnamed x128 -> x124, local copies, waits for them, and re-layouts: 15 us -> 17.7 us
    dot_general x6, matrix products: 8.07 us -> 5.62 us  [matmul_tn(): lax.dot_general(left, right, (((0,), (0,)), ((), ())), preferred_element_...]
  transfers between devices with their start and end apart: 31 -> 31, of which waited for: 18 -> 18; matrix products, arithmetic and copies ran while one was open for 29% -> 33% of each run, Pallas kernels for 0% -> 0%
where the time goes in v4:
time: 200 us; the launch traced here: 199 us
  waiting for transfers between devices  78 us (39%)
  starting transfers between devices  38.7 us (19%)
  matrix products  30.1 us (15%)
  local copies, waits for them, and re-layouts  26.4 us (13%)
  other arithmetic  24.3 us (12%)
    ppermute x31, waiting for transfers between devices, swap(): return lax.ppermute(value, axis, pairs)  78 us
    ppermute x31, starting transfers between devices, swap(): return lax.ppermute(value, axis, pairs)  38.7 us
    unnamed x124, local copies, waits for them, and re-layouts  17.7 us
    dot_general x7, matrix products, matmul(): return jnp.dot(left, right, preferred_element_type=jnp.float32)  10.9 us
    dot_general x4, matrix products, matmul_nt(): lax.dot_general(left, right, (((1,), (1,)), ((), ())), preferred_element_...  8.7 us
    dot_general x6, matrix products, matmul_tn(): lax.dot_general(left, right, (((0,), (0,)), ((), ())), preferred_element_...  5.62 us
  transfers between devices with their start and end apart: 31, of which 18 were waited for; matrix products, arithmetic and copies ran while one was open for 33% of the time, Pallas kernels for 0%

profile of v4, /device:TPU:0, one launch (start us, length us, event | category | flops | bytes accessed | tf_op | source)
XLA Modules:
  0.0 199.4 jit_solution(8830632965064895723)
XLA Ops:
  0.7 2.5 %convolution_convert_fusion.3 = bf16[1024,256]{1,0:T(8,128)(2,1)S(1)} fusion(bf16[1024,1024]{1,0:T(8,128)(2,1)} %bitcast.149, bf16[3,1024,256]{2,1,0:T(8,128)(2,1)} %param.15), kind=kOutput, calls=%fused_computation.23 | convolution fusion | flops 537133056 | bytes 3145728 | tf_op jit(solution)/shard_map/dot_general | solution.py:10
  13.6 1.7 slice_dynamic-update-slice_fusion.5
  19.3 1.7 slice_dynamic-update-slice_fusion.2
  21.1 2.6 %collective-permute-start.1 = (bf16[128,1024]{1,0:T(8,128)(2,1)S(1)}, bf16[128,1024]{1,0:T(8,128)(2,1)S(1)}, u32[]{:S(2)}, u32[]{:S(2)}) collective-permute-start(bf16[128,1024]{1,0:T(8,128)(2,1)S(1)} %add_convert_fusion.5), channel_id=1, source_target_pairs={{0,2},{1,3},{2,0},{3,1},{4,6},{5,7},{6,4},{7,5},{8,10},{9,11},{10,... | collective-permute-start | bytes 786440 | tf_op jit(solution)/shard_map/ppermute | solution.py:50
  26.6 4.1 %collective-permute-done.1 = bf16[128,1024]{1,0:T(8,128)(2,1)S(1)} collective-permute-done((bf16[128,1024]{1,0:T(8,128)(2,1)S(1)}, bf16[128,1024]{1,0:T(8,128)(2,1)S(1)}, u32[]{:S(2)}, u32[]{:S(2)}) %collective-permute-start.1) | collective-permute-done | bytes 262176 | tf_op jit(solution)/shard_map/ppermute | solution.py:50
  38.9 1.8 collective-permute-start.4
  41.7 2.7 %collective-permute-start.21 = (bf16[128,1280]{1,0:T(8,128)(2,1)S(1)}, bf16[128,1280]{1,0:T(8,128)(2,1)S(1)}, u32[]{:S(2)}, u32[]{:S(2)}) collective-permute-start(bf16[128,1280]{1,0:T(8,128)(2,1)S(1)} %maximum_maximum_fusion.1), channel_id=1, source_target_pairs={{0,16},{4,20},{8,24},{12,28},{16,0},{20,4},{24,8},{28,12},{1,17},{... | collective-permute-start | bytes 983048 | tf_op jit(solution)/shard_map/ppermute | solution.py:50
  44.8 2.8 %collective-permute-done.4 = bf16[128,1024]{1,0:T(8,128)(2,1)S(1)} collective-permute-done((bf16[128,1024]{1,0:T(8,128)(2,1)S(1)}, bf16[128,1024]{1,0:T(8,128)(2,1)S(1)}, u32[]{:S(2)}, u32[]{:S(2)}) %collective-permute-start.4) | collective-permute-done | bytes 262176 | tf_op jit(solution)/shard_map/ppermute | solution.py:50
  48.8 6.3 %fusion.103 = (f32[128]{0:T(128)S(1)}, f32[128,4096]{1,0:T(8,128)S(1)}) fusion(bf16[128,1024]{1,0:T(8,128)(2,1)S(1)} %multiply_convert_fusion, bf16[4096,1024]{1,0:T(8,128)(2,1)} %param.19), kind=kOutput, calls=%fused_computation.287 | convolution fusion | flops 1074265984 | bytes 10748416 | tf_op jit(solution)/shard_map/dot_general | solution.py:20
  56.0 9.9 %collective-permute-done.21 = bf16[128,1280]{1,0:T(8,128)(2,1)S(1)} collective-permute-done((bf16[128,1280]{1,0:T(8,128)(2,1)S(1)}, bf16[128,1280]{1,0:T(8,128)(2,1)S(1)}, u32[]{:S(2)}, u32[]{:S(2)}) %collective-permute-start.21) | collective-permute-done | bytes 327712 | tf_op jit(solution)/shard_map/ppermute | solution.py:50
  67.4 3.5 %collective-permute-done.2 = bf16[2,128,512]{2,1,0:T(8,128)(2,1)S(1)} collective-permute-done((bf16[2,128,512]{2,1,0:T(8,128)(2,1)S(1)}, bf16[2,128,512]{2,1,0:T(8,128)(2,1)S(1)}, u32[]{:S(2)}, u32[]{:S(2)}) %collective-permute-start.2) | collective-permute-done | bytes 262176 | tf_op jit(solution)/shard_map/ppermute | solution.py:50
  82.8 5.5 %convolution_convert_fusion.6 = bf16[128,1024]{1,0:T(8,128)(2,1)S(1)} fusion(bf16[4096,1024]{1,0:T(8,128)(2,1)} %param.19, f32[128,4096]{1,0:T(8,128)} %copy-done.1, f32[128]{0:T(128)S(1)} %get-tuple-element.94, s32[128]{0:T(128)S(1)} %copy-done.38), kind=kOutput, calls=%fused_computation.27 | convolution fusion | flops 1076494336 | bytes 10748928 | tf_op jit(solution)/shard_map/dot_general | solution.py:10
  89.1 3.0 %collective-permute-done.12 = f32[2,2]{1,0:T(2,128)S(1)} collective-permute-done((f32[2,2]{1,0:T(2,128)S(1)}, f32[2,2]{1,0:T(2,128)S(1)}, u32[]{:S(2)}, u32[]{:S(2)}) %collective-permute-start.12) | collective-permute-done | bytes 48 | tf_op jit(solution)/shard_map/ppermute | solution.py:50
  92.1 2.1 %collective-permute-start.13 = (f32[2,2]{1,0:T(2,128)S(1)}, f32[2,2]{1,0:T(2,128)S(1)}, u32[]{:S(2)}, u32[]{:S(2)}) collective-permute-start(f32[2,2]{1,0:T(2,128)S(1)} %log_add_fusion.1), channel_id=1, source_target_pairs={{0,16},{4,20},{8,24},{12,28},{16,0},{20,4},{24,8},{28,12},{1,17},{... | collective-permute-start | bytes 56 | tf_op jit(solution)/shard_map/ppermute | solution.py:50
  94.2 2.4 %collective-permute-done.13 = f32[2,2]{1,0:T(2,128)S(1)} collective-permute-done((f32[2,2]{1,0:T(2,128)S(1)}, f32[2,2]{1,0:T(2,128)S(1)}, u32[]{:S(2)}, u32[]{:S(2)}) %collective-permute-start.13) | collective-permute-done | bytes 48 | tf_op jit(solution)/shard_map/ppermute | solution.py:50
  102.1 2.2 %collective-permute-done.10 = bf16[128,1024]{1,0:T(8,128)(2,1)} collective-permute-done((bf16[128,1024]{1,0:T(8,128)(2,1)}, bf16[128,1024]{1,0:T(8,128)(2,1)}, u32[]{:S(2)}, u32[]{:S(2)}) %collective-permute-start.10) | collective-permute-done | bytes 262176 | tf_op jit(solution)/shard_map/ppermute | solution.py:50
  110.1 2.1 %collective-permute-start.19 = (bf16[128,1024]{1,0:T(8,128)(2,1)S(1)}, bf16[128,1024]{1,0:T(8,128)(2,1)S(1)}, u32[]{:S(2)}, u32[]{:S(2)}) collective-permute-start(bf16[128,1024]{1,0:T(8,128)(2,1)S(1)} %fusion.28), channel_id=1, source_target_pairs={{0,16},{4,20},{8,24},{12,28},{16,0},{20,4},{24,8},{28,12},{1,17},{... | collective-permute-start | bytes 786440 | tf_op jit(solution)/shard_map/ppermute | solution.py:50
  116.4 4.2 %collective-permute-done.15 = bf16[128,1024]{1,0:T(8,128)(2,1)S(1)} collective-permute-done((bf16[128,1024]{1,0:T(8,128)(2,1)S(1)}, bf16[128,1024]{1,0:T(8,128)(2,1)S(1)}, u32[]{:S(2)}, u32[]{:S(2)}) %collective-permute-start.15) | collective-permute-done | bytes 262176 | tf_op jit(solution)/shard_map/ppermute | solution.py:50
  122.9 2.8 %fusion.13 = bf16[4,128,512]{2,1,0:T(8,128)(2,1)S(1)} fusion(f32[4,128,512]{2,1,0:T(8,128)S(1)} %fusion.63, f32[4,128,512]{2,1,0:T(8,128)S(1)} %copy-done.53, f32[4,128]{1,0:T(4,128)S(1)} %copy-done.55), kind=kOutput, calls=%fused_computation.24 | output fusion | flops 1836031 | bytes 2623488 | tf_op jit(solution)/shard_map/sub | solution.py:267
  127.8 1.8 collective-permute-start.20
  129.7 2.3 %collective-permute-start.16 = (bf16[128,256]{1,0:T(8,128)(2,1)S(1)}, bf16[128,256]{1,0:T(8,128)(2,1)S(1)}, u32[]{:S(2)}, u32[]{:S(2)}) collective-permute-start(bf16[128,256]{1,0:T(8,128)(2,1)S(1)} %maximum_maximum_fusion.2), channel_id=1, source_target_pairs={{0,16},{4,20},{8,24},{12,28},{16,0},{20,4},{24,8},{28,12},{1,17},{... | collective-permute-start | bytes 196616 | tf_op jit(solution)/shard_map/ppermute | solution.py:50
  132.3 12.7 %collective-permute-done.16 = bf16[128,256]{1,0:T(8,128)(2,1)S(1)} collective-permute-done((bf16[128,256]{1,0:T(8,128)(2,1)S(1)}, bf16[128,256]{1,0:T(8,128)(2,1)S(1)}, u32[]{:S(2)}, u32[]{:S(2)}) %collective-permute-start.16) | collective-permute-done | bytes 65568 | tf_op jit(solution)/shard_map/ppermute | solution.py:50
  145.0 4.8 %collective-permute-start.17 = (bf16[256,256]{1,0:T(8,128)(2,1)S(1)}, bf16[256,256]{1,0:T(8,128)(2,1)S(1)}, u32[]{:S(2)}, u32[]{:S(2)}) collective-permute-start(bf16[256,256]{1,0:T(8,128)(2,1)S(1)} %pad_maximum_fusion.12), channel_id=1, source_target_pairs={{0,8},{4,12},{8,0},{12,4},{16,24},{20,28},{24,16},{28,20},{1,9},{5... | collective-permute-start | bytes 393224 | tf_op jit(solution)/shard_map/ppermute | solution.py:50
  149.8 2.9 %collective-permute-done.17 = bf16[256,256]{1,0:T(8,128)(2,1)S(1)} collective-permute-done((bf16[256,256]{1,0:T(8,128)(2,1)S(1)}, bf16[256,256]{1,0:T(8,128)(2,1)S(1)}, u32[]{:S(2)}, u32[]{:S(2)}) %collective-permute-start.17) | collective-permute-done | bytes 131104 | tf_op jit(solution)/shard_map/ppermute | solution.py:50
  157.8 2.1 %collective-permute-start.28 = (bf16[2,256,256]{2,1,0:T(8,128)(2,1)S(1)}, bf16[2,256,256]{2,1,0:T(8,128)(2,1)S(1)}, u32[]{:S(2)}, u32[]{:S(2)}) collective-permute-start(bf16[2,256,256]{2,1,0:T(8,128)(2,1)S(1)} %get-tuple-element.41), channel_id=1, source_target_pairs={{0,8},{4,12},{8,0},{12,4},{16,24},{20,28},{24,16},{28,20},{1,9},{5... | collective-permute-start | bytes 786440 | tf_op jit(solution)/shard_map/ppermute | solution.py:50
  159.9 2.0 %collective-permute-done.18 = bf16[512,256]{1,0:T(8,128)(2,1)S(1)} collective-permute-done((bf16[512,256]{1,0:T(8,128)(2,1)S(1)}, bf16[512,256]{1,0:T(8,128)(2,1)S(1)}, u32[]{:S(2)}, u32[]{:S(2)}) %collective-permute-start.18) | collective-permute-done | bytes 262176 | tf_op jit(solution)/shard_map/ppermute | solution.py:50
  162.2 2.0 %collective-permute-done.28 = bf16[2,256,256]{2,1,0:T(8,128)(2,1)S(1)} collective-permute-done((bf16[2,256,256]{2,1,0:T(8,128)(2,1)S(1)}, bf16[2,256,256]{2,1,0:T(8,128)(2,1)S(1)}, u32[]{:S(2)}, u32[]{:S(2)}) %collective-permute-start.28) | collective-permute-done | bytes 262176 | tf_op jit(solution)/shard_map/ppermute | solution.py:50
  166.4 6.7 %collective-permute-done.24 = bf16[512,512]{1,0:T(8,128)(2,1)S(1)} collective-permute-done((bf16[512,512]{1,0:T(8,128)(2,1)S(1)}, bf16[512,512]{1,0:T(8,128)(2,1)S(1)}, u32[]{:S(2)}, u32[]{:S(2)}) %collective-permute-start.24) | collective-permute-done | bytes 524320 | tf_op jit(solution)/shard_map/ppermute | solution.py:50
  173.9 2.1 %collective-permute-start.25 = (bf16[256,512]{1,0:T(8,128)(2,1)S(1)}, bf16[256,512]{1,0:T(8,128)(2,1)S(1)}, u32[]{:S(2)}, u32[]{:S(2)}) collective-permute-start(bf16[256,512]{1,0:T(8,128)(2,1)S(1)} %dynamic-slice_convert_fusion), channel_id=1, source_target_pairs={{0,8},{4,12},{8,0},{12,4},{16,24},{20,28},{24,16},{28,20},{1,9},{5... | collective-permute-start | bytes 786440 | tf_op jit(solution)/shard_map/ppermute | solution.py:50
  176.1 2.7 %collective-permute-done.29 = bf16[2,512,128]{2,1,0:T(8,128)(2,1)S(1)} collective-permute-done((bf16[2,512,128]{2,1,0:T(8,128)(2,1)S(1)}, bf16[2,512,128]{2,1,0:T(8,128)(2,1)S(1)}, u32[]{:S(2)}, u32[]{:S(2)}) %collective-permute-start.29) | collective-permute-done | bytes 262176 | tf_op jit(solution)/shard_map/ppermute | solution.py:50
  183.6 5.7 %collective-permute-done.26 = bf16[128,512]{1,0:T(8,128)(2,1)S(1)} collective-permute-done((bf16[128,512]{1,0:T(8,128)(2,1)S(1)}, bf16[128,512]{1,0:T(8,128)(2,1)S(1)}, u32[]{:S(2)}, u32[]{:S(2)}) %collective-permute-start.26) | collective-permute-done | bytes 131104 | tf_op jit(solution)/shard_map/ppermute | solution.py:50
  190.1 8.0 %collective-permute-done.30 = bf16[512,1024]{1,0:T(8,128)(2,1)S(1)} collective-permute-done((bf16[512,1024]{1,0:T(8,128)(2,1)S(1)}, bf16[512,1024]{1,0:T(8,128)(2,1)S(1)}, u32[]{:S(2)}, u32[]{:S(2)}) %collective-permute-start.30) | collective-permute-done | bytes 1048608 | tf_op jit(solution)/shard_map/ppermute | solution.py:50
  (271 shorter events, 77.8 us)
Async XLA Ops:
  0.6 31.8 %copy-start = (bf16[1024,1024]{1,0:T(8,128)(2,1)S(1)}, bf16[1024,1024]{1,0:T(8,128)(2,1)}, u32[]{:S(2)}) copy-start(bf16[1024,1024]{1,0:T(8,128)(2,1)} %param.17) | copy-start | bytes 6291460
  9.6 11.4 %collective-permute-start = (bf16[128,1024]{1,0:T(8,128)(2,1)S(1)}, bf16[128,1024]{1,0:T(8,128)(2,1)S(1)}, u32[]{:S(2)}, u32[]{:S(2)}) collective-permute-start(bf16[128,1024]{1,0:T(8,128)(2,1)S(1)} %convolution_convert_fusion.8), channel_id=1, source_target_pairs={{0,1},{1,0},{2,3},{3,2},{4,5},{5,4},{6,7},{7,6},{8,9},{9,8},{10,11... | collective-permute-start | bytes 786440 | tf_op jit(solution)/shard_map/ppermute | solution.py:50
  21.1 9.6 %collective-permute-start.1 = (bf16[128,1024]{1,0:T(8,128)(2,1)S(1)}, bf16[128,1024]{1,0:T(8,128)(2,1)S(1)}, u32[]{:S(2)}, u32[]{:S(2)}) collective-permute-start(bf16[128,1024]{1,0:T(8,128)(2,1)S(1)} %add_convert_fusion.5), channel_id=1, source_target_pairs={{0,2},{1,3},{2,0},{3,1},{4,6},{5,7},{6,4},{7,5},{8,10},{9,11},{10,... | collective-permute-start | bytes 786440 | tf_op jit(solution)/shard_map/ppermute | solution.py:50
  34.3 3.6 %collective-permute-start.3 = (bf16[128,1024]{1,0:T(8,128)(2,1)S(1)}, bf16[128,1024]{1,0:T(8,128)(2,1)}, u32[]{:S(2)}, u32[]{:S(2)}) collective-permute-start(bf16[128,1024]{1,0:T(8,128)(2,1)S(1)} %convolution_convert_fusion.7), channel_id=1, source_target_pairs={{0,1},{1,0},{2,3},{3,2},{4,5},{5,4},{6,7},{7,6},{8,9},{9,8},{10,11... | collective-permute-start | bytes 786440 | tf_op jit(solution)/shard_map/ppermute | solution.py:50
  38.9 8.8 %collective-permute-start.4 = (bf16[128,1024]{1,0:T(8,128)(2,1)S(1)}, bf16[128,1024]{1,0:T(8,128)(2,1)S(1)}, u32[]{:S(2)}, u32[]{:S(2)}) collective-permute-start(bf16[128,1024]{1,0:T(8,128)(2,1)S(1)} %add_convert_fusion.4), channel_id=1, source_target_pairs={{0,2},{1,3},{2,0},{3,1},{4,6},{5,7},{6,4},{7,5},{8,10},{9,11},{10,... | collective-permute-start | bytes 786440 | tf_op jit(solution)/shard_map/ppermute | solution.py:50
  41.7 24.1 %collective-permute-start.21 = (bf16[128,1280]{1,0:T(8,128)(2,1)S(1)}, bf16[128,1280]{1,0:T(8,128)(2,1)S(1)}, u32[]{:S(2)}, u32[]{:S(2)}) collective-permute-start(bf16[128,1280]{1,0:T(8,128)(2,1)S(1)} %maximum_maximum_fusion.1), channel_id=1, source_target_pairs={{0,16},{4,20},{8,24},{12,28},{16,0},{20,4},{24,8},{28,12},{1,17},{... | collective-permute-start | bytes 983048 | tf_op jit(solution)/shard_map/ppermute | solution.py:50
  44.4 26.4 %collective-permute-start.2 = (bf16[2,128,512]{2,1,0:T(8,128)(2,1)S(1)}, bf16[2,128,512]{2,1,0:T(8,128)(2,1)S(1)}, u32[]{:S(2)}, u32[]{:S(2)}) collective-permute-start(bf16[2,128,512]{2,1,0:T(8,128)(2,1)S(1)} %get-tuple-element.49), channel_id=1, source_target_pairs={{0,16},{4,20},{8,24},{12,28},{16,0},{20,4},{24,8},{28,12},{1,17},{... | collective-permute-start | bytes 786440 | tf_op jit(solution)/shard_map/ppermute | solution.py:50
  55.9 15.1 %collective-permute-start.6 = (f32[2,128]{1,0:T(2,128)S(1)}, f32[2,128]{1,0:T(2,128)S(1)}, u32[]{:S(2)}, u32[]{:S(2)}) collective-permute-start(f32[2,128]{1,0:T(2,128)S(1)} %pad_maximum_fusion.31), channel_id=1, source_target_pairs={{0,1},{1,0},{2,3},{3,2},{4,5},{5,4},{6,7},{7,6},{8,9},{9,8},{10,11... | collective-permute-start | bytes 3080 | tf_op jit(solution)/shard_map/ppermute | solution.py:50
  67.4 44.9 %collective-permute-start.22 = (bf16[256,1280]{1,0:T(8,128)(2,1)}, bf16[256,1280]{1,0:T(8,128)(2,1)}, u32[]{:S(2)}, u32[]{:S(2)}) collective-permute-start(bf16[256,1280]{1,0:T(8,128)(2,1)} %constant_dynamic-update-slice_fusion.9), channel_id=1, source_target_pairs={{0,8},{4,12},{8,0},{12,4},{16,24},{20,28},{24,16},{28,20},{1,9},{5... | collective-permute-start | bytes 1966088 | tf_op jit(solution)/shard_map/ppermute | solution.py:50
  71.0 3.6 %collective-permute-start.7 = (f32[2,128]{1,0:T(2,128)S(1)}, f32[2,128]{1,0:T(2,128)S(1)}, u32[]{:S(2)}, u32[]{:S(2)}) collective-permute-start(f32[2,128]{1,0:T(2,128)S(1)} %add_select_fusion.2), channel_id=1, source_target_pairs={{0,2},{1,3},{2,0},{3,1},{4,6},{5,7},{6,4},{7,5},{8,10},{9,11},{10,... | collective-permute-start | bytes 3080 | tf_op jit(solution)/shard_map/ppermute | solution.py:50
  72.3 27.7 %collective-permute-start.5 = (bf16[2,256,256]{2,1,0:T(8,128)(2,1)}, bf16[2,256,256]{2,1,0:T(8,128)(2,1)}, u32[]{:S(2)}, u32[]{:S(2)}) collective-permute-start(bf16[2,256,256]{2,1,0:T(8,128)(2,1)} %get-tuple-element.47), channel_id=1, source_target_pairs={{0,8},{4,12},{8,0},{12,4},{16,24},{20,28},{24,16},{28,20},{1,9},{5... | collective-permute-start | bytes 786440 | tf_op jit(solution)/shard_map/ppermute | solution.py:50
  81.3 7.1 %collective-permute-start.11 = (f32[2,2]{1,0:T(2,128)S(1)}, f32[2,2]{1,0:T(2,128)S(1)}, u32[]{:S(2)}, u32[]{:S(2)}) collective-permute-start(f32[2,2]{1,0:T(2,128)S(1)} %add_select_fusion), channel_id=1, source_target_pairs={{0,4},{4,0},{8,12},{12,8},{16,20},{20,16},{24,28},{28,24},{1,5},{5... | collective-permute-start | bytes 56 | tf_op jit(solution)/shard_map/ppermute | solution.py:50
  88.3 8.5 %collective-permute-start.9 = (bf16[128,1024]{1,0:T(8,128)(2,1)S(1)}, bf16[128,1024]{1,0:T(8,128)(2,1)S(1)}, u32[]{:S(2)}, u32[]{:S(2)}) collective-permute-start(bf16[128,1024]{1,0:T(8,128)(2,1)S(1)} %convolution_convert_fusion.6), channel_id=1, source_target_pairs={{0,1},{1,0},{2,3},{3,2},{4,5},{5,4},{6,7},{7,6},{8,9},{9,8},{10,11... | collective-permute-start | bytes 786440 | tf_op jit(solution)/shard_map/ppermute | solution.py:50
  88.4 3.6 %collective-permute-start.12 = (f32[2,2]{1,0:T(2,128)S(1)}, f32[2,2]{1,0:T(2,128)S(1)}, u32[]{:S(2)}, u32[]{:S(2)}) collective-permute-start(f32[2,2]{1,0:T(2,128)S(1)} %log_add_fusion.2), channel_id=1, source_target_pairs={{0,8},{4,12},{8,0},{12,4},{16,24},{20,28},{24,16},{28,20},{1,9},{5... | collective-permute-start | bytes 56 | tf_op jit(solution)/shard_map/ppermute | solution.py:50
  92.1 4.5 %collective-permute-start.13 = (f32[2,2]{1,0:T(2,128)S(1)}, f32[2,2]{1,0:T(2,128)S(1)}, u32[]{:S(2)}, u32[]{:S(2)}) collective-permute-start(f32[2,2]{1,0:T(2,128)S(1)} %log_add_fusion.1), channel_id=1, source_target_pairs={{0,16},{4,20},{8,24},{12,28},{16,0},{20,4},{24,8},{28,12},{1,17},{... | collective-permute-start | bytes 56 | tf_op jit(solution)/shard_map/ppermute | solution.py:50
  97.6 6.7 %collective-permute-start.10 = (bf16[128,1024]{1,0:T(8,128)(2,1)}, bf16[128,1024]{1,0:T(8,128)(2,1)}, u32[]{:S(2)}, u32[]{:S(2)}) collective-permute-start(bf16[128,1024]{1,0:T(8,128)(2,1)} %add_convert_fusion.3), channel_id=1, source_target_pairs={{0,2},{1,3},{2,0},{3,1},{4,6},{5,7},{6,4},{7,5},{8,10},{9,11},{10,... | collective-permute-start | bytes 786440 | tf_op jit(solution)/shard_map/ppermute | solution.py:50
  109.1 3.2 %collective-permute-start.14 = (bf16[128,1024]{1,0:T(8,128)(2,1)S(1)}, bf16[128,1024]{1,0:T(8,128)(2,1)S(1)}, u32[]{:S(2)}, u32[]{:S(2)}) collective-permute-start(bf16[128,1024]{1,0:T(8,128)(2,1)S(1)} %convolution_convert_fusion.5), channel_id=1, source_target_pairs={{0,1},{1,0},{2,3},{3,2},{4,5},{5,4},{6,7},{7,6},{8,9},{9,8},{10,11... | collective-permute-start | bytes 786440 | tf_op jit(solution)/shard_map/ppermute | solution.py:50
  109.3 52.6 %collective-permute-start.8 = (bf16[2,512,128]{2,1,0:T(8,128)(2,1)S(1)}, bf16[2,512,128]{2,1,0:T(8,128)(2,1)S(1)}, u32[]{:S(2)}, u32[]{:S(2)}) collective-permute-start(bf16[2,512,128]{2,1,0:T(8,128)(2,1)S(1)} %get-tuple-element.45), channel_id=1, source_target_pairs={{0,4},{4,0},{8,12},{12,8},{16,20},{20,16},{24,28},{28,24},{1,5},{5... | collective-permute-start | bytes 786440 | tf_op jit(solution)/shard_map/ppermute | solution.py:50
  110.1 17.7 %collective-permute-start.19 = (bf16[128,1024]{1,0:T(8,128)(2,1)S(1)}, bf16[128,1024]{1,0:T(8,128)(2,1)S(1)}, u32[]{:S(2)}, u32[]{:S(2)}) collective-permute-start(bf16[128,1024]{1,0:T(8,128)(2,1)S(1)} %fusion.28), channel_id=1, source_target_pairs={{0,16},{4,20},{8,24},{12,28},{16,0},{20,4},{24,8},{28,12},{1,17},{... | collective-permute-start | bytes 786440 | tf_op jit(solution)/shard_map/ppermute | solution.py:50
  112.4 8.2 %collective-permute-start.15 = (bf16[128,1024]{1,0:T(8,128)(2,1)S(1)}, bf16[128,1024]{1,0:T(8,128)(2,1)S(1)}, u32[]{:S(2)}, u32[]{:S(2)}) collective-permute-start(bf16[128,1024]{1,0:T(8,128)(2,1)S(1)} %add_convert_fusion.1), channel_id=1, source_target_pairs={{0,2},{1,3},{2,0},{3,1},{4,6},{5,7},{6,4},{7,5},{8,10},{9,11},{10,... | collective-permute-start | bytes 786440 | tf_op jit(solution)/shard_map/ppermute | solution.py:50
  114.9 39.5 %collective-permute-start.23 = (bf16[512,1280]{1,0:T(8,128)(2,1)S(1)}, bf16[512,1280]{1,0:T(8,128)(2,1)S(1)}, u32[]{:S(2)}, u32[]{:S(2)}) collective-permute-start(bf16[512,1280]{1,0:T(8,128)(2,1)S(1)} %pad_maximum_fusion.1), channel_id=1, source_target_pairs={{0,4},{4,0},{8,12},{12,8},{16,20},{20,16},{24,28},{28,24},{1,5},{5... | collective-permute-start | bytes 3932168 | tf_op jit(solution)/shard_map/ppermute | solution.py:50
  126.4 31.3 %collective-permute-start.27 = (bf16[2,128,512]{2,1,0:T(8,128)(2,1)S(1)}, bf16[2,128,512]{2,1,0:T(8,128)(2,1)S(1)}, u32[]{:S(2)}, u32[]{:S(2)}) collective-permute-start(bf16[2,128,512]{2,1,0:T(8,128)(2,1)S(1)} %get-tuple-element.43), channel_id=1, source_target_pairs={{0,16},{4,20},{8,24},{12,28},{16,0},{20,4},{24,8},{28,12},{1,17},{... | collective-permute-start | bytes 786440 | tf_op jit(solution)/shard_map/ppermute | solution.py:50
  127.8 26.4 %collective-permute-start.20 = (bf16[256,1024]{1,0:T(8,128)(2,1)S(1)}, bf16[256,1024]{1,0:T(8,128)(2,1)S(1)}, u32[]{:S(2)}, u32[]{:S(2)}) collective-permute-start(bf16[256,1024]{1,0:T(8,128)(2,1)S(1)} %pad_maximum_fusion.5), channel_id=1, source_target_pairs={{0,8},{4,12},{8,0},{12,4},{16,24},{20,28},{24,16},{28,20},{1,9},{5... | collective-permute-start | bytes 1572872 | tf_op jit(solution)/shard_map/ppermute | solution.py:50
  129.7 15.3 %collective-permute-start.16 = (bf16[128,256]{1,0:T(8,128)(2,1)S(1)}, bf16[128,256]{1,0:T(8,128)(2,1)S(1)}, u32[]{:S(2)}, u32[]{:S(2)}) collective-permute-start(bf16[128,256]{1,0:T(8,128)(2,1)S(1)} %maximum_maximum_fusion.2), channel_id=1, source_target_pairs={{0,16},{4,20},{8,24},{12,28},{16,0},{20,4},{24,8},{28,12},{1,17},{... | collective-permute-start | bytes 196616 | tf_op jit(solution)/shard_map/ppermute | solution.py:50
  145.0 7.7 %collective-permute-start.17 = (bf16[256,256]{1,0:T(8,128)(2,1)S(1)}, bf16[256,256]{1,0:T(8,128)(2,1)S(1)}, u32[]{:S(2)}, u32[]{:S(2)}) collective-permute-start(bf16[256,256]{1,0:T(8,128)(2,1)S(1)} %pad_maximum_fusion.12), channel_id=1, source_target_pairs={{0,8},{4,12},{8,0},{12,4},{16,24},{20,28},{24,16},{28,20},{1,9},{5... | collective-permute-start | bytes 393224 | tf_op jit(solution)/shard_map/ppermute | solution.py:50
  152.7 9.2 %collective-permute-start.18 = (bf16[512,256]{1,0:T(8,128)(2,1)S(1)}, bf16[512,256]{1,0:T(8,128)(2,1)S(1)}, u32[]{:S(2)}, u32[]{:S(2)}) collective-permute-start(bf16[512,256]{1,0:T(8,128)(2,1)S(1)} %pad_maximum_fusion.9), channel_id=1, source_target_pairs={{0,4},{4,0},{8,12},{12,8},{16,20},{20,16},{24,28},{28,24},{1,5},{5... | collective-permute-start | bytes 786440 | tf_op jit(solution)/shard_map/ppermute | solution.py:50
  157.1 16.0 %collective-permute-start.24 = (bf16[512,512]{1,0:T(8,128)(2,1)S(1)}, bf16[512,512]{1,0:T(8,128)(2,1)S(1)}, u32[]{:S(2)}, u32[]{:S(2)}) collective-permute-start(bf16[512,512]{1,0:T(8,128)(2,1)S(1)} %convolution_convert_fusion.4), channel_id=1, source_target_pairs={{0,4},{4,0},{8,12},{12,8},{16,20},{20,16},{24,28},{28,24},{1,5},{5... | collective-permute-start | bytes 1572872 | tf_op jit(solution)/shard_map/ppermute | solution.py:50
  157.8 6.4 %collective-permute-start.28 = (bf16[2,256,256]{2,1,0:T(8,128)(2,1)S(1)}, bf16[2,256,256]{2,1,0:T(8,128)(2,1)S(1)}, u32[]{:S(2)}, u32[]{:S(2)}) collective-permute-start(bf16[2,256,256]{2,1,0:T(8,128)(2,1)S(1)} %get-tuple-element.41), channel_id=1, source_target_pairs={{0,8},{4,12},{8,0},{12,4},{16,24},{20,28},{24,16},{28,20},{1,9},{5... | collective-permute-start | bytes 786440 | tf_op jit(solution)/shard_map/ppermute | solution.py:50
  164.3 14.4 %collective-permute-start.29 = (bf16[2,512,128]{2,1,0:T(8,128)(2,1)S(1)}, bf16[2,512,128]{2,1,0:T(8,128)(2,1)S(1)}, u32[]{:S(2)}, u32[]{:S(2)}) collective-permute-start(bf16[2,512,128]{2,1,0:T(8,128)(2,1)S(1)} %get-tuple-element.39), channel_id=1, source_target_pairs={{0,4},{4,0},{8,12},{12,8},{16,20},{20,16},{24,28},{28,24},{1,5},{5... | collective-permute-start | bytes 786440 | tf_op jit(solution)/shard_map/ppermute | solution.py:50
  165.9 32.2 %collective-permute-start.30 = (bf16[512,1024]{1,0:T(8,128)(2,1)S(1)}, bf16[512,1024]{1,0:T(8,128)(2,1)S(1)}, u32[]{:S(2)}, u32[]{:S(2)}) collective-permute-start(bf16[512,1024]{1,0:T(8,128)(2,1)S(1)} %pad_maximum_fusion.2), channel_id=1, source_target_pairs={{0,4},{4,0},{8,12},{12,8},{16,20},{20,16},{24,28},{28,24},{1,5},{5... | collective-permute-start | bytes 3145736 | tf_op jit(solution)/shard_map/ppermute | solution.py:50
  173.9 7.9 %collective-permute-start.25 = (bf16[256,512]{1,0:T(8,128)(2,1)S(1)}, bf16[256,512]{1,0:T(8,128)(2,1)S(1)}, u32[]{:S(2)}, u32[]{:S(2)}) collective-permute-start(bf16[256,512]{1,0:T(8,128)(2,1)S(1)} %dynamic-slice_convert_fusion), channel_id=1, source_target_pairs={{0,8},{4,12},{8,0},{12,4},{16,24},{20,28},{24,16},{28,20},{1,9},{5... | collective-permute-start | bytes 786440 | tf_op jit(solution)/shard_map/ppermute | solution.py:50
  181.9 7.3 %collective-permute-start.26 = (bf16[128,512]{1,0:T(8,128)(2,1)S(1)}, bf16[128,512]{1,0:T(8,128)(2,1)S(1)}, u32[]{:S(2)}, u32[]{:S(2)}) collective-permute-start(bf16[128,512]{1,0:T(8,128)(2,1)S(1)} %dynamic-slice_convert_fusion.1), channel_id=1, source_target_pairs={{0,16},{4,20},{8,24},{12,28},{16,0},{20,4},{24,8},{28,12},{1,17},{... | collective-permute-start | bytes 393224 | tf_op jit(solution)/shard_map/ppermute | solution.py:50
  (55 other events, 267.5 us)
